TPU v7x, 128 devices: a whole 4x4x4 slice. The times are simulated.
128 devices in a mesh: dom: 128 (over y, z, x, core).
Axes of the slice: x: 4, y: 4, z: 4, core: 2. Of those that a mesh axis runs over, the one named last changes fastest.
Arguments:
- thickness: float32 [16, 262144], P(None, 'dom'), may hold values from 0.5 to 1.5
- velocity: float32 [16, 786432], P(None, 'dom'), may hold values from -4 to 4
- send_cells: int32 [512, 256], P('dom'), may hold values from 0 to 2047
- send_edges: int32 [512, 512], P('dom'), may hold values from 0 to 6143
- cell_edges: int32 [6, 262144], P(None, 'dom'), may hold values from 0 to 8191
- cell_orient: int32 [6, 262144], P(None, 'dom'), may hold values from 0 to 1
- edge_cells: int32 [2, 786432], P(None, 'dom'), may hold values from 0 to 3071
- edge_edges: int32 [10, 786432], P(None, 'dom'), may hold values from 0 to 8191
- edge_weights: float32 [10, 786432], P(None, 'dom'), may hold values from -2 to 2
- cell_area: float32 [262144], P('dom'), may hold values from 2 to 6
- edge_spacing: float32 [786432], P('dom'), may hold values from 0.5 to 2
- edge_length: float32 [786432], P('dom'), may hold values from 0.5 to 2
- coriolis: float32 [786432], P('dom'), may hold values from 0.5 to 1.5
Outputs:
- new_thickness: float32 [16, 262144], P(None, 'dom')
- new_velocity: float32 [16, 786432], P(None, 'dom')
Inputs may be any that keep to these rules, and one draw needn't show every extreme that they name: `cell_edges`: extended local edge numbers, owned edges first, then halo slots in order of j. `edge_cells`: extended local cell numbers, owned cells first, then halo slots in order of j.
All inputs are finite; a program needn't handle non-finite values.
Results may differ from a plain program's by a relative error of at most 0.0001.
Values sent between devices are 32-bit elements; how exact they have to be, the bound alone decides.
A program may use at most 128 MiB of HBM per device.

v0:
```python
import jax
import jax.numpy as jnp
from jax import lax
from jax.sharding import PartitionSpec as P

gravity = 0.1
mixing = 0.2
time_step = 0.5


def shifted(block, axis, distance):
    devices = range(lax.axis_size(axis))
    route = [(i - distance, i) for i in devices if i - distance in devices]
    return lax.ppermute(block, axis, route)


def peer_offsets(slot_count):
    half = slot_count // 2
    return [place - half if place < half else place - half + 1 for place in range(slot_count)]


def state_halo(cell_blocks, edge_blocks):
    slot_count = cell_blocks.shape[0]
    offsets = peer_offsets(slot_count)
    arrived = {}
    for place, offset in enumerate(offsets):
        arrived[offset] = shifted((cell_blocks[place], edge_blocks[place]), "dom", offset)
    cell_parts = [arrived[offset][0] for offset in offsets]
    edge_parts = [arrived[offset][1] for offset in offsets]
    return (jnp.concatenate(cell_parts, axis=0), jnp.concatenate(edge_parts, axis=0))


def flux_halo(flux_blocks):
    slot_count = flux_blocks.shape[0]
    offsets = peer_offsets(slot_count)
    arrived = {}
    for place, offset in enumerate(offsets):
        arrived[offset] = shifted(flux_blocks[place], "dom", offset)
    return jnp.concatenate([arrived[offset] for offset in offsets], axis=0)


def shards(
    thickness,
    velocity,
    send_cells,
    send_edges,
    cell_edges,
    cell_orient,
    edge_cells,
    edge_edges,
    edge_weights,
    cell_area,
    edge_spacing,
    edge_length,
    coriolis,
):
    levels = thickness.shape[0]
    edge_count = velocity.shape[1]
    cell_count = thickness.shape[1]
    signs = (2 * cell_orient - 1).astype(jnp.float32).T
    pair_index = edge_cells.reshape(-1)
    around_index = edge_edges.reshape(-1)
    side_index = cell_edges.T.reshape(-1)
    rows_h0 = thickness.T
    rows_u0 = velocity.T
    rows_h = rows_h0
    rows_u = rows_u0
    for section in range(3):
        step_size = time_step / (3 - section)
        cell_blocks = jnp.take(rows_h, send_cells, axis=0)
        edge_blocks = jnp.take(rows_u, send_edges, axis=0)
        halo_h, halo_u = state_halo(cell_blocks, edge_blocks)
        ext_h = jnp.concatenate([rows_h, halo_h], axis=0)
        ext_u = jnp.concatenate([rows_u, halo_u], axis=0)
        ext_p = gravity * (jnp.cumsum(ext_h, axis=1) - 0.5 * ext_h)
        table = jnp.concatenate([ext_h, ext_p], axis=1)
        picked = jnp.take(table, pair_index, axis=0).reshape(2, edge_count, 2 * levels)
        left_h = picked[0, :, :levels]
        right_h = picked[1, :, :levels]
        gradient = (picked[1, :, levels:] - picked[0, :, levels:]) / edge_spacing[:, None]
        beside_all = jnp.take(ext_u, around_index, axis=0).reshape(-1, edge_count, levels)
        tangent = jnp.sum(beside_all * edge_weights[:, :, None], axis=0)
        upper = jnp.concatenate([rows_u[:, :1], rows_u[:, :-1]], axis=1)
        lower = jnp.concatenate([rows_u[:, 1:], rows_u[:, -1:]], axis=1)
        blend = mixing * (upper + lower - 2.0 * rows_u)
        u_next = rows_u0 + step_size * (-gradient + coriolis[:, None] * tangent + blend)
        flux = u_next * 0.5 * (left_h + right_h) * edge_length[:, None]
        halo_f = flux_halo(jnp.take(flux, send_edges, axis=0))
        ext_f = jnp.concatenate([flux, halo_f], axis=0)
        sides = jnp.take(ext_f, side_index, axis=0).reshape(cell_count, -1, levels)
        spread = jnp.sum(sides * signs[:, :, None], axis=1)
        rows_h = rows_h0 - step_size * spread / cell_area[:, None]
        rows_u = u_next
    return (rows_h.T, rows_u.T)


def solution(mesh):
    return jax.shard_map(
        shards,
        mesh=mesh,
        in_specs=(
            P(None, "dom"),
            P(None, "dom"),
            P("dom", None),
            P("dom", None),
            P(None, "dom"),
            P(None, "dom"),
            P(None, "dom"),
            P(None, "dom"),
            P(None, "dom"),
            P("dom"),
            P("dom"),
            P("dom"),
            P("dom"),
        ),
        out_specs=(P(None, "dom"), P(None, "dom")),
        check_vma=False,
    )
```

profile of v0, /device:TPU:9, one launch (start us, length us, event | category | flops | bytes accessed | tf_op | source)
XLA Modules:
  0.0 1512.2 jit_solution(12341664125058514106)
XLA Ops:
  63.8 41.1 %gather_fusion.1 = f32[12288,32]{1,0:T(8,128)} fusion(f32[3072,32]{1,0:T(8,128)S(1)} %copy.215, s32[12288]{0:T(1024)S(1)} %fusion.25), kind=kCustom, calls=%fused_computation.1.clone | custom fusion | bytes 3194880 | tf_op jit(solution)/shard_map/jit(_take)/gather | solution.py:77
  104.9 8.6 broadcast_select_fusion.8
  139.8 224.0 %gather_fusion.3 = f32[61440,16]{1,0:T(8,128)} fusion(f32[8192,16]{1,0:T(8,128)} %copy.222, s32[61440]{0:T(1024)} %fusion.24), kind=kCustom, calls=%fused_computation.3.clone | custom fusion | bytes 8110080 | tf_op jit(solution)/shard_map/jit(_take)/gather | solution.py:81
  363.8 34.4 %broadcast_select_fusion.2 = f32[61440,16]{1,0:T(8,128)} fusion(f32[61440,16]{1,0:T(8,128)} %gather_fusion.3, pred[61440]{0:T(1024)(128)(4,1)S(1)} %copy-done.26), kind=kLoop, calls=%fused_computation.23 | loop fusion | flops 983040 | bytes 7925760 | tf_op jit(solution)/shard_map/jit(_take)/select_n | solution.py:81
  398.2 11.4 multiply_reduce_fusion.2
  421.8 9.4 gather_fusion.4
  441.9 12.7 collective-permute-start.8
  492.2 43.2 %gather_fusion.5 = f32[12288,16]{1,0:T(8,128)} fusion(f32[8192,16]{1,0:T(8,128)} %copy.229, s32[12288]{0:T(1024)S(1)} %copy-done.29), kind=kCustom, calls=%fused_computation.4.clone | custom fusion | bytes 1622016 | tf_op jit(solution)/shard_map/jit(_take)/gather | solution.py:90
  535.5 10.3 broadcast_select_fusion.5
  545.8 8.5 reshape.82
  554.4 12.6 multiply_reduce_fusion.5
  583.0 7.9 collective-permute-start.12
  593.6 204.4 %gather_fusion.9 = f32[61440,16]{1,0:T(8,128)} fusion(f32[8192,16]{1,0:T(8,128)} %copy.242, s32[61440]{0:T(1024)S(1)} %copy-done.11), kind=kCustom, calls=%fused_computation.14.clone | custom fusion | bytes 8110080 | tf_op jit(solution)/shard_map/jit(_take)/gather | solution.py:81
  798.0 34.4 %broadcast_select_fusion.1 = f32[61440,16]{1,0:T(8,128)} fusion(f32[61440,16]{1,0:T(8,128)} %gather_fusion.9, pred[61440]{0:T(1024)(128)(4,1)S(1)} %copy-done.27), kind=kLoop, calls=%fused_computation.22 | loop fusion | flops 983040 | bytes 7925760 | tf_op jit(solution)/shard_map/jit(_take)/select_n | solution.py:81
  832.4 11.4 multiply_reduce_fusion.1
  846.4 41.1 %gather_fusion.7 = f32[12288,32]{1,0:T(8,128)} fusion(f32[3072,32]{1,0:T(8,128)S(1)} %copy.235, s32[12288]{0:T(1024)S(1)} %copy-done.33), kind=kCustom, calls=%fused_computation.7.clone | custom fusion | bytes 3194880 | tf_op jit(solution)/shard_map/jit(_take)/gather | solution.py:77
  887.5 8.6 broadcast_select_fusion.7
  922.1 9.4 gather_fusion.10
  983.2 43.2 %gather_fusion.11 = f32[12288,16]{1,0:T(8,128)} fusion(f32[8192,16]{1,0:T(8,128)} %copy.249, s32[12288]{0:T(1024)S(1)} %copy-done.30), kind=kCustom, calls=%fused_computation.16.clone | custom fusion | bytes 1622016 | tf_op jit(solution)/shard_map/jit(_take)/gather | solution.py:90
  1026.4 10.3 broadcast_select_fusion.4
  1036.7 8.5 reshape.85
  1045.3 12.6 multiply_reduce_fusion.4
  1074.0 8.1 collective-permute-start.24
  1084.8 204.4 %gather_fusion.15 = f32[61440,16]{1,0:T(8,128)} fusion(f32[8192,16]{1,0:T(8,128)} %copy.261, s32[61440]{0:T(1024)S(1)} %copy-done.12), kind=kCustom, calls=%fused_computation.15.clone | custom fusion | bytes 8110080 | tf_op jit(solution)/shard_map/jit(_take)/gather | solution.py:81
  1289.2 34.4 %broadcast_select_fusion = f32[61440,16]{1,0:T(8,128)} fusion(f32[61440,16]{1,0:T(8,128)} %gather_fusion.15, pred[61440]{0:T(1024)(128)(4,1)S(1)} %copy-done.28), kind=kLoop, calls=%fused_computation.21 | loop fusion | flops 983040 | bytes 7925760 | tf_op jit(solution)/shard_map/jit(_take)/select_n | solution.py:81
  1323.6 11.4 multiply_reduce_fusion
  1337.6 41.1 %gather_fusion.13 = f32[12288,32]{1,0:T(8,128)} fusion(f32[3072,32]{1,0:T(8,128)S(1)} %copy.254, s32[12288]{0:T(1024)S(1)} %copy-done.34), kind=kCustom, calls=%fused_computation.8.clone | custom fusion | bytes 3194880 | tf_op jit(solution)/shard_map/jit(_take)/gather | solution.py:77
  1378.7 8.6 broadcast_select_fusion.6
  1435.9 43.2 %gather_fusion.17 = f32[12288,16]{1,0:T(8,128)} fusion(f32[8192,16]{1,0:T(8,128)} %copy.268, s32[12288]{0:T(1024)S(1)} %copy-done.31), kind=kCustom, calls=%fused_computation.17.clone | custom fusion | bytes 1622016 | tf_op jit(solution)/shard_map/jit(_take)/gather | solution.py:90
  1479.2 10.3 broadcast_select_fusion.3
  1489.5 8.5 reshape.88
  1498.0 12.6 multiply_reduce_fusion.3
  (347 shorter events, 318.8 us)
Async XLA Ops:
  7.0 55.3 %collective-permute-start.3 = (f32[256,16]{0,1:T(8,128)}, f32[256,16]{0,1:T(8,128)}, u32[]{:S(2)}, u32[]{:S(2)}) collective-permute-start(f32[256,16]{0,1:T(8,128)} %get-tuple-element.86), channel_id=1, source_target_pairs={{0,2},{1,3},{2,4},{3,5},{4,6},{5,7},{6,8},{7,9},{8,10},{9,11},{10,... | collective-permute-start | bytes 49160 | tf_op jit(solution)/shard_map/ppermute | solution.py:14
  10.1 44.0 %collective-permute-start.2 = (f32[256,16]{0,1:T(8,128)}, f32[256,16]{0,1:T(8,128)}, u32[]{:S(2)}, u32[]{:S(2)}) collective-permute-start(f32[256,16]{0,1:T(8,128)} %get-tuple-element.87), channel_id=1, source_target_pairs={{0,1},{1,2},{2,3},{3,4},{4,5},{5,6},{6,7},{7,8},{8,9},{9,10},{10,1... | collective-permute-start | bytes 49160 | tf_op jit(solution)/shard_map/ppermute | solution.py:14
  14.1 37.0 %collective-permute-start.1 = (f32[256,16]{0,1:T(8,128)}, f32[256,16]{0,1:T(8,128)}, u32[]{:S(2)}, u32[]{:S(2)}) collective-permute-start(f32[256,16]{0,1:T(8,128)} %get-tuple-element.88), channel_id=1, source_target_pairs={{1,0},{2,1},{3,2},{4,3},{5,4},{6,5},{7,6},{8,7},{9,8},{10,9},{11,1... | collective-permute-start | bytes 49160 | tf_op jit(solution)/shard_map/ppermute | solution.py:14
  16.0 30.5 %collective-permute-start = (f32[256,16]{0,1:T(8,128)}, f32[256,16]{0,1:T(8,128)}, u32[]{:S(2)}, u32[]{:S(2)}) collective-permute-start(f32[256,16]{0,1:T(8,128)} %get-tuple-element.89), channel_id=1, source_target_pairs={{2,0},{3,1},{4,2},{5,3},{6,4},{7,5},{8,6},{9,7},{10,8},{11,9},{12,... | collective-permute-start | bytes 49160 | tf_op jit(solution)/shard_map/ppermute | solution.py:14
  33.3 101.6 %collective-permute-start.7 = (f32[512,16]{0,1:T(8,128)}, f32[512,16]{0,1:T(8,128)}, u32[]{:S(2)}, u32[]{:S(2)}) collective-permute-start(f32[512,16]{0,1:T(8,128)} %get-tuple-element.74), channel_id=1, source_target_pairs={{0,2},{1,3},{2,4},{3,5},{4,6},{5,7},{6,8},{7,9},{8,10},{9,11},{10,... | collective-permute-start | bytes 98312 | tf_op jit(solution)/shard_map/ppermute | solution.py:14
  46.5 87.1 %collective-permute-start.6 = (f32[512,16]{0,1:T(8,128)}, f32[512,16]{0,1:T(8,128)}, u32[]{:S(2)}, u32[]{:S(2)}) collective-permute-start(f32[512,16]{0,1:T(8,128)} %get-tuple-element.75), channel_id=1, source_target_pairs={{0,1},{1,2},{2,3},{3,4},{4,5},{5,6},{6,7},{7,8},{8,9},{9,10},{10,1... | collective-permute-start | bytes 98312 | tf_op jit(solution)/shard_map/ppermute | solution.py:14
  51.1 81.1 %collective-permute-start.5 = (f32[512,16]{0,1:T(8,128)}, f32[512,16]{0,1:T(8,128)}, u32[]{:S(2)}, u32[]{:S(2)}) collective-permute-start(f32[512,16]{0,1:T(8,128)} %get-tuple-element.76), channel_id=1, source_target_pairs={{1,0},{2,1},{3,2},{4,3},{5,4},{6,5},{7,6},{8,7},{9,8},{10,9},{11,1... | collective-permute-start | bytes 98312 | tf_op jit(solution)/shard_map/ppermute | solution.py:14
  54.1 76.7 %collective-permute-start.4 = (f32[512,16]{0,1:T(8,128)}, f32[512,16]{0,1:T(8,128)}, u32[]{:S(2)}, u32[]{:S(2)}) collective-permute-start(f32[512,16]{0,1:T(8,128)} %get-tuple-element.77), channel_id=1, source_target_pairs={{2,0},{3,1},{4,2},{5,3},{6,4},{7,5},{8,6},{9,7},{10,8},{11,9},{12,... | collective-permute-start | bytes 98312 | tf_op jit(solution)/shard_map/ppermute | solution.py:14
  441.9 28.7 %collective-permute-start.8 = (f32[512,16]{0,1:T(8,128)S(1)}, f32[512,16]{0,1:T(8,128)S(1)}, u32[]{:S(2)}, u32[]{:S(2)}) collective-permute-start(f32[512,16]{0,1:T(8,128)S(1)} %get-tuple-element.73), channel_id=1, source_target_pairs={{2,0},{3,1},{4,2},{5,3},{6,4},{7,5},{8,6},{9,7},{10,8},{11,9},{12,... | collective-permute-start | bytes 98312 | tf_op jit(solution)/shard_map/ppermute | solution.py:14
  454.6 136.3 %collective-permute-start.19 = (f32[512,16]{0,1:T(8,128)S(1)}, f32[512,16]{0,1:T(8,128)S(1)}, u32[]{:S(2)}, u32[]{:S(2)}) collective-permute-start(f32[512,16]{0,1:T(8,128)S(1)} %get-tuple-element.66), channel_id=1, source_target_pairs={{0,2},{1,3},{2,4},{3,5},{4,6},{5,7},{6,8},{7,9},{8,10},{9,11},{10,... | collective-permute-start | bytes 98312 | tf_op jit(solution)/shard_map/ppermute | solution.py:14
  457.7 125.3 %collective-permute-start.18 = (f32[512,16]{0,1:T(8,128)S(1)}, f32[512,16]{0,1:T(8,128)S(1)}, u32[]{:S(2)}, u32[]{:S(2)}) collective-permute-start(f32[512,16]{0,1:T(8,128)S(1)} %get-tuple-element.67), channel_id=1, source_target_pairs={{0,1},{1,2},{2,3},{3,4},{4,5},{5,6},{6,7},{7,8},{8,9},{9,10},{10,1... | collective-permute-start | bytes 98312 | tf_op jit(solution)/shard_map/ppermute | solution.py:14
  462.2 114.2 %collective-permute-start.17 = (f32[512,16]{0,1:T(8,128)S(1)}, f32[512,16]{0,1:T(8,128)S(1)}, u32[]{:S(2)}, u32[]{:S(2)}) collective-permute-start(f32[512,16]{0,1:T(8,128)S(1)} %get-tuple-element.68), channel_id=1, source_target_pairs={{1,0},{2,1},{3,2},{4,3},{5,4},{6,5},{7,6},{8,7},{9,8},{10,9},{11,1... | collective-permute-start | bytes 98312 | tf_op jit(solution)/shard_map/ppermute | solution.py:14
  464.2 109.1 %collective-permute-start.16 = (f32[512,16]{0,1:T(8,128)S(1)}, f32[512,16]{0,1:T(8,128)S(1)}, u32[]{:S(2)}, u32[]{:S(2)}) collective-permute-start(f32[512,16]{0,1:T(8,128)S(1)} %get-tuple-element.69), channel_id=1, source_target_pairs={{2,0},{3,1},{4,2},{5,3},{6,4},{7,5},{8,6},{9,7},{10,8},{11,9},{12,... | collective-permute-start | bytes 98312 | tf_op jit(solution)/shard_map/ppermute | solution.py:14
  479.2 8.9 collective-permute-start.11
  571.3 274.4 %collective-permute-start.15 = (f32[256,16]{0,1:T(8,128)S(1)}, f32[256,16]{0,1:T(8,128)S(1)}, u32[]{:S(2)}, u32[]{:S(2)}) collective-permute-start(f32[256,16]{0,1:T(8,128)S(1)} %get-tuple-element.82), channel_id=1, source_target_pairs={{0,2},{1,3},{2,4},{3,5},{4,6},{5,7},{6,8},{7,9},{8,10},{9,11},{10,... | collective-permute-start | bytes 49160 | tf_op jit(solution)/shard_map/ppermute | solution.py:14
  573.2 272.4 %collective-permute-start.14 = (f32[256,16]{0,1:T(8,128)S(1)}, f32[256,16]{0,1:T(8,128)S(1)}, u32[]{:S(2)}, u32[]{:S(2)}) collective-permute-start(f32[256,16]{0,1:T(8,128)S(1)} %get-tuple-element.83), channel_id=1, source_target_pairs={{0,1},{1,2},{2,3},{3,4},{4,5},{5,6},{6,7},{7,8},{8,9},{9,10},{10,1... | collective-permute-start | bytes 49160 | tf_op jit(solution)/shard_map/ppermute | solution.py:14
  576.5 269.1 %collective-permute-start.13 = (f32[256,16]{0,1:T(8,128)}, f32[256,16]{0,1:T(8,128)S(1)}, u32[]{:S(2)}, u32[]{:S(2)}) collective-permute-start(f32[256,16]{0,1:T(8,128)} %get-tuple-element.84), channel_id=1, source_target_pairs={{1,0},{2,1},{3,2},{4,3},{5,4},{6,5},{7,6},{8,7},{9,8},{10,9},{11,1... | collective-permute-start | bytes 49160 | tf_op jit(solution)/shard_map/ppermute | solution.py:14
  583.0 262.6 %collective-permute-start.12 = (f32[256,16]{0,1:T(8,128)}, f32[256,16]{0,1:T(8,128)S(1)}, u32[]{:S(2)}, u32[]{:S(2)}) collective-permute-start(f32[256,16]{0,1:T(8,128)} %get-tuple-element.85), channel_id=1, source_target_pairs={{2,0},{3,1},{4,2},{5,3},{6,4},{7,5},{8,6},{9,7},{10,8},{11,9},{12,... | collective-permute-start | bytes 49160 | tf_op jit(solution)/shard_map/ppermute | solution.py:14
  942.2 19.3 %collective-permute-start.20 = (f32[512,16]{0,1:T(8,128)S(1)}, f32[512,16]{0,1:T(8,128)S(1)}, u32[]{:S(2)}, u32[]{:S(2)}) collective-permute-start(f32[512,16]{0,1:T(8,128)S(1)} %get-tuple-element.65), channel_id=1, source_target_pairs={{2,0},{3,1},{4,2},{5,3},{6,4},{7,5},{8,6},{9,7},{10,8},{11,9},{12,... | collective-permute-start | bytes 98312 | tf_op jit(solution)/shard_map/ppermute | solution.py:14
  945.5 136.6 %collective-permute-start.31 = (f32[512,16]{0,1:T(8,128)S(1)}, f32[512,16]{0,1:T(8,128)S(1)}, u32[]{:S(2)}, u32[]{:S(2)}) collective-permute-start(f32[512,16]{0,1:T(8,128)S(1)} %get-tuple-element.58), channel_id=1, source_target_pairs={{0,2},{1,3},{2,4},{3,5},{4,6},{5,7},{6,8},{7,9},{8,10},{9,11},{10,... | collective-permute-start | bytes 98312 | tf_op jit(solution)/shard_map/ppermute | solution.py:14
  947.6 126.4 %collective-permute-start.30 = (f32[512,16]{0,1:T(8,128)S(1)}, f32[512,16]{0,1:T(8,128)S(1)}, u32[]{:S(2)}, u32[]{:S(2)}) collective-permute-start(f32[512,16]{0,1:T(8,128)S(1)} %get-tuple-element.59), channel_id=1, source_target_pairs={{0,1},{1,2},{2,3},{3,4},{4,5},{5,6},{6,7},{7,8},{8,9},{9,10},{10,1... | collective-permute-start | bytes 98312 | tf_op jit(solution)/shard_map/ppermute | solution.py:14
  951.7 115.7 %collective-permute-start.29 = (f32[512,16]{0,1:T(8,128)S(1)}, f32[512,16]{0,1:T(8,128)S(1)}, u32[]{:S(2)}, u32[]{:S(2)}) collective-permute-start(f32[512,16]{0,1:T(8,128)S(1)} %get-tuple-element.60), channel_id=1, source_target_pairs={{1,0},{2,1},{3,2},{4,3},{5,4},{6,5},{7,6},{8,7},{9,8},{10,9},{11,1... | collective-permute-start | bytes 98312 | tf_op jit(solution)/shard_map/ppermute | solution.py:14
  954.0 110.2 %collective-permute-start.28 = (f32[512,16]{0,1:T(8,128)S(1)}, f32[512,16]{0,1:T(8,128)S(1)}, u32[]{:S(2)}, u32[]{:S(2)}) collective-permute-start(f32[512,16]{0,1:T(8,128)S(1)} %get-tuple-element.61), channel_id=1, source_target_pairs={{2,0},{3,1},{4,2},{5,3},{6,4},{7,5},{8,6},{9,7},{10,8},{11,9},{12,... | collective-permute-start | bytes 98312 | tf_op jit(solution)/shard_map/ppermute | solution.py:14
  970.1 8.9 collective-permute-start.23
  1062.2 274.6 %collective-permute-start.27 = (f32[256,16]{0,1:T(8,128)S(1)}, f32[256,16]{0,1:T(8,128)S(1)}, u32[]{:S(2)}, u32[]{:S(2)}) collective-permute-start(f32[256,16]{0,1:T(8,128)S(1)} %get-tuple-element.78), channel_id=1, source_target_pairs={{0,2},{1,3},{2,4},{3,5},{4,6},{5,7},{6,8},{7,9},{8,10},{9,11},{10,... | collective-permute-start | bytes 49160 | tf_op jit(solution)/shard_map/ppermute | solution.py:14
  1064.2 272.7 %collective-permute-start.26 = (f32[256,16]{0,1:T(8,128)S(1)}, f32[256,16]{0,1:T(8,128)S(1)}, u32[]{:S(2)}, u32[]{:S(2)}) collective-permute-start(f32[256,16]{0,1:T(8,128)S(1)} %get-tuple-element.79), channel_id=1, source_target_pairs={{0,1},{1,2},{2,3},{3,4},{4,5},{5,6},{6,7},{7,8},{8,9},{9,10},{10,1... | collective-permute-start | bytes 49160 | tf_op jit(solution)/shard_map/ppermute | solution.py:14
  1067.4 269.4 %collective-permute-start.25 = (f32[256,16]{0,1:T(8,128)}, f32[256,16]{0,1:T(8,128)S(1)}, u32[]{:S(2)}, u32[]{:S(2)}) collective-permute-start(f32[256,16]{0,1:T(8,128)} %get-tuple-element.80), channel_id=1, source_target_pairs={{1,0},{2,1},{3,2},{4,3},{5,4},{6,5},{7,6},{8,7},{9,8},{10,9},{11,1... | collective-permute-start | bytes 49160 | tf_op jit(solution)/shard_map/ppermute | solution.py:14
  1074.0 262.8 %collective-permute-start.24 = (f32[256,16]{0,1:T(8,128)}, f32[256,16]{0,1:T(8,128)S(1)}, u32[]{:S(2)}, u32[]{:S(2)}) collective-permute-start(f32[256,16]{0,1:T(8,128)} %get-tuple-element.81), channel_id=1, source_target_pairs={{2,0},{3,1},{4,2},{5,3},{6,4},{7,5},{8,6},{9,7},{10,8},{11,9},{12,... | collective-permute-start | bytes 49160 | tf_op jit(solution)/shard_map/ppermute | solution.py:14
  1415.6 12.0 collective-permute-start.32
  1418.8 12.9 collective-permute-start.35
  1420.9 10.2 collective-permute-start.34
  1425.0 5.5 collective-permute-start.33
  (67 other events, 2082.6 us)
where the time goes:
time: 1530 us; the launch traced here: 1510 us
  local copies, waits for them, and re-layouts  1100 us (72%)
  other arithmetic  249 us (16%)
  starting transfers between devices  142 us (9%)
  waiting for transfers between devices  21.2 us (1%)
    gather x3, local copies, waits for them, and re-layouts, shards(): jnp.take(ext_u, around_index, axis=0).reshape(-1, edge_count, levels)  633 us
    ppermute x36, starting transfers between devices, shifted(): return lax.ppermute(block, axis, route)  142 us
    gather x3, local copies, waits for them, and re-layouts, shards(): sides = jnp.take(ext_f, side_index, axis=0).reshape(cell_count, -1, levels)  130 us
    gather x3, local copies, waits for them, and re-layouts, shards(): jnp.take(table, pair_index, axis=0).reshape(2, edge_count, 2 * levels)  123 us
    select_n x3, other arithmetic, shards(): jnp.take(ext_u, around_index, axis=0).reshape(-1, edge_count, levels)  103 us
    unnamed x170, local copies, waits for them, and re-layouts  45.7 us
    reduce_sum x3, other arithmetic, shards(): spread = jnp.sum(sides * signs[:, :, None], axis=1)  37.9 us
    reduce_sum x3, other arithmetic, shards(): tangent = jnp.sum(beside_all * edge_weights[:, :, None], axis=0)  34.1 us
  transfers between devices with their start and end apart: 36, of which 7 were waited for; matrix products, arithmetic and copies ran while one was open for 51% of the time, Pallas kernels for 0%

commit v1 on v0

v1 whole, which is shorter than its diff:
```python
import functools

import jax
import jax.numpy as jnp
from jax import lax
from jax.experimental import pallas as pl
from jax.experimental.pallas import tpu as pltpu
from jax.sharding import PartitionSpec as P

gravity = 0.1
mixing = 0.2
time_step = 0.5
LANES = 128
BLOCK = 32
STEP = 8
OFFSETS = (-2, -1, 1, 2)
VMEM = pltpu.VMEM
SMEM = pltpu.SMEM


class Plan:
    def __init__(self, terms, octets, chunks, cap, weighted):
        self.terms, self.octets, self.chunks, self.cap, self.weighted = terms, octets, chunks, cap, weighted

    def shapes(self):
        blocks = self.octets * self.cap // BLOCK
        raw = (self.terms, self.octets * 8, LANES)
        out = [
            jax.ShapeDtypeStruct(raw, jnp.int32),
            jax.ShapeDtypeStruct((self.octets * self.cap, LANES), jnp.int32),
            jax.ShapeDtypeStruct((-(-blocks // 8) * 8, LANES), jnp.int32),
            jax.ShapeDtypeStruct((self.octets,), jnp.int32),
        ]
        if self.weighted:
            out += [
                jax.ShapeDtypeStruct(raw, jnp.float32),
                jax.ShapeDtypeStruct((self.octets * self.cap, LANES), jnp.float32),
            ]
        return out

    def out_specs(self):
        spaces = [VMEM, VMEM, VMEM, SMEM] + [VMEM, VMEM] * self.weighted
        return [pl.BlockSpec(memory_space=s) for s in spaces]

    def in_specs(self):
        spaces = [VMEM, VMEM, SMEM, SMEM] + [VMEM, VMEM] * self.weighted
        return [pl.BlockSpec(memory_space=s) for s in spaces]

    def count(self):
        return 6 if self.weighted else 4


AROUND = Plan(10, 6, 64, 384, True)
PAIR = Plan(1, 12, 24, 96, False)
SIDE = Plan(6, 2, 64, 320, True)
SEND_E = Plan(1, 2, 48, 128, False)
SEND_C = Plan(1, 1, 16, 64, False)


def iota(axis):
    return lax.broadcasted_iota(jnp.int32, (8, LANES), axis)


def spread_row(ref, *at):
    return jnp.broadcast_to(ref[at], (8, LANES))


def build(plan, refs, keys, loads):
    raw, packed, chunk_of, counts = refs[:4]
    sub, lane = iota(0), iota(1)

    def octet(o, carry):
        at = pl.ds(pl.multiple_of(o * 8, 8), 8)
        chunk = [lax.shift_right_logical(raw[k, at, :], 7) for k in range(plan.terms)]
        base = jnp.zeros((8, LANES), jnp.int32)
        key = [jnp.zeros((8, LANES), jnp.int32) for _ in range(plan.terms)]
        for c in range(plan.chunks):
            hit = [chunk[k] == c for k in range(plan.terms)]
            one = [h.astype(jnp.int32) for h in hit]
            total = one[0]
            for k in range(1, plan.terms):
                total = total + one[k]
            upto = total
            for shift in (1, 2, 4):
                upto = upto + jnp.where(sub >= shift, pltpu.roll(upto, shift, 0), 0)
            rounds = jnp.max(jnp.max(upto, axis=1, keepdims=True), axis=0, keepdims=True)
            start = base + upto - total
            for k in range(plan.terms):
                key[k] = jnp.where(hit[k], start, key[k])
                if k + 1 < plan.terms:
                    start = start + one[k]
            base = base + rounds
        number = base[0, 0]
        counts[o] = number
        for k in range(plan.terms):
            keys[k] = key[k]
            loads[k] = (raw[k, at, :] & 127) | (sub << 7) | (chunk[k] << 11)

        def block(b, carry):
            row = [sub + (b * BLOCK + 8 * v) for v in range(BLOCK // 8)]
            load = [jnp.full((8, LANES), 8 << 7, jnp.int32) for _ in row]
            weight = [jnp.zeros((8, LANES), jnp.float32) for _ in row]
            for k in range(plan.terms):
                for s in range(8):
                    wanted = spread_row(keys, k, pl.ds(s, 1), slice(None))
                    value = spread_row(loads, k, pl.ds(s, 1), slice(None))
                    if plan.weighted:
                        scale = spread_row(refs[4], k, pl.ds(o * 8 + s, 1), slice(None))
                    for v in range(BLOCK // 8):
                        here = wanted == row[v]
                        load[v] = jnp.where(here, value, load[v])
                        if plan.weighted:
                            weight[v] = jnp.where(here, scale, weight[v])
            ids = jnp.zeros((8, LANES), jnp.int32)
            for v in range(BLOCK // 8):
                to = pl.ds(pl.multiple_of(o * plan.cap + b * BLOCK + 8 * v, 8), 8)
                packed[to, :] = load[v] & 2047
                if plan.weighted:
                    refs[5][to, :] = weight[v]
                own = jnp.max(load[v] >> 11, axis=1, keepdims=True)
                ids = ids + jnp.where(lane == sub + 8 * v, own, 0)
            chunk_of[pl.ds(o * (plan.cap // BLOCK) + b, 1), :] = jnp.sum(ids, axis=0, keepdims=True)
            return carry

        lax.fori_loop(0, (jnp.minimum(number, plan.cap) + BLOCK - 1) // BLOCK, block, 0)
        return carry

    lax.fori_loop(0, plan.octets, octet, 0)


def lanes_at(position):
    return pl.ds(pl.multiple_of(position * LANES, LANES), LANES)


def gather(plan, refs, o, sources, put, add):
    raw, packed, chunk_of, counts = refs[:4]
    number = counts[o]
    total = 8 * len(sources)
    empty = tuple(jnp.zeros((8, LANES), jnp.float32) for _ in range(total))

    def finish(sums):
        for d in range(8):
            for i in range(len(sources)):
                put(d, i, sums[d * len(sources) + i])

    @pl.when(number <= plan.cap)
    def _():
        def step(t, sums):
            sums = list(sums)
            for r in range(STEP):
                row = t * STEP + r
                c = chunk_of[o * (plan.cap // BLOCK) + row // BLOCK, row % BLOCK]
                at = o * plan.cap + row
                load = spread_row(packed, pl.ds(at, 1), slice(None))
                pick, goal = load & 127, lax.shift_right_logical(load, 7)
                if plan.weighted:
                    scale = spread_row(refs[5], pl.ds(at, 1), slice(None))
                values = []
                for ref, rows in sources:
                    value = jnp.take_along_axis(ref[rows, lanes_at(c)], pick, axis=1, mode="promise_in_bounds")
                    values.append(value * scale if plan.weighted else value)
                for d in range(8):
                    mine = goal == d
                    for i, value in enumerate(values):
                        j = d * len(sources) + i
                        sums[j] = sums[j] + jnp.where(mine, value, 0.0) if add else jnp.where(mine, value, sums[j])
            return tuple(sums)

        finish(lax.fori_loop(0, (number + STEP - 1) // STEP, step, empty))

    @pl.when(number > plan.cap)
    def _():
        for d in range(8):
            sums = tuple(jnp.zeros((8, LANES), jnp.float32) for _ in sources)
            for k in range(plan.terms):
                index = spread_row(raw, k, pl.ds(o * 8 + d, 1), slice(None))
                pick, chunk = index & 127, lax.shift_right_logical(index, 7)

                def look(c, found):
                    out = []
                    for (ref, rows), old in zip(sources, found):
                        value = jnp.take_along_axis(ref[rows, lanes_at(c)], pick, axis=1, mode="promise_in_bounds")
                        out.append(jnp.where(chunk == c, value, old))
                    return tuple(out)

                found = lax.fori_loop(0, plan.chunks, look, tuple(jnp.zeros((8, LANES), jnp.float32) for _ in sources))
                if plan.weighted:
                    scale = spread_row(refs[4], k, pl.ds(o * 8 + d, 1), slice(None))
                    found = tuple(f * scale for f in found)
                sums = tuple(s + f for s, f in zip(sums, found))
            for i in range(len(sources)):
                put(d, i, sums[i])


TOP, LOW = slice(0, 8), slice(8, 16)


def both(*refs):
    return [(ref, rows) for ref in refs for rows in (TOP, LOW)]


def sends_kernel(h, u, send_c, send_e, *rest):
    plan_e, plan_c, (out, keys, loads, ids_e, ids_c) = rest[:4], rest[4:8], rest[8:]
    for j in range(4):
        for q in range(4):
            plan_e[0][0, 4 * j + q : 4 * j + q + 1, :] = send_e[j : j + 1, q * LANES : (q + 1) * LANES]
        for q in range(2):
            plan_c[0][0, 2 * j + q : 2 * j + q + 1, :] = send_c[j : j + 1, q * LANES : (q + 1) * LANES]
    build(SEND_E, plan_e, keys, loads)
    build(SEND_C, plan_c, keys, loads)
    pltpu.sync_copy(plan_e[2], ids_e)
    pltpu.sync_copy(plan_c[2], ids_c)
    plan_e = (*plan_e[:2], ids_e, plan_e[3])
    plan_c = (*plan_c[:2], ids_c, plan_c[3])
    for o in range(2):

        def put_u(d, i, value):
            j, q = (o * 8 + d) // 4, (o * 8 + d) % 4
            out[8 * i : 8 * i + 8, j * 768 + q * LANES : j * 768 + (q + 1) * LANES] = value

        gather(SEND_E, plan_e, o, both(u), put_u, False)

    def put_h(d, i, value):
        j, q = d // 2, d % 2
        out[8 * i : 8 * i + 8, j * 768 + 512 + q * LANES : j * 768 + 512 + (q + 1) * LANES] = value

    gather(SEND_C, plan_c, 0, both(h), put_h, False)


def plans_kernel(edge_edges, edge_weights, edge_cells, cell_edges, cell_orient, *rest):
    around, pair, side = rest[:6], rest[6:10], rest[10:16]
    keys, loads = rest[16:]
    for g in range(48):
        at = slice(g * LANES, (g + 1) * LANES)
        for k in range(10):
            around[0][k, g : g + 1, :] = edge_edges[k : k + 1, at]
            around[4][k, g : g + 1, :] = edge_weights[k : k + 1, at]
        for k in range(2):
            to = g // 4 * 8 + k * 4 + g % 4
            pair[0][0, to : to + 1, :] = edge_cells[k : k + 1, at]
    for g in range(16):
        at = slice(g * LANES, (g + 1) * LANES)
        for k in range(6):
            side[0][k, g : g + 1, :] = cell_edges[k : k + 1, at]
            side[4][k, g : g + 1, :] = (2 * cell_orient[k : k + 1, at] - 1).astype(jnp.float32)
    build(AROUND, around, keys, loads)
    build(PAIR, pair, keys, loads)
    build(SIDE, side, keys, loads)


def below(x, shift):
    return pltpu.roll(x, shift, 0)


def edge_kernel(tau, last, u_place, h_place, *refs):
    velocity, u_own, h_own, halo_u, halo_h, spacing, length, coriolis = refs[:8]
    around, pair, refs = refs[8:14], refs[14:18], refs[18:]
    send_e, (u_next, flux, out, ext_u, ext_h, tangent, cells) = refs[:4], refs[4:]
    ext_u[:, : 48 * LANES] = u_own[...]
    ext_h[:, : 16 * LANES] = h_own[...]
    for j in range(4):
        at = j * u_place[0] + u_place[1]
        ext_u[:, 48 * LANES + 512 * j : 48 * LANES + 512 * (j + 1)] = halo_u[:, at : at + 512]
        at = j * h_place[0] + h_place[1]
        ext_h[:, 16 * LANES + 256 * j : 16 * LANES + 256 * (j + 1)] = halo_h[:, at : at + 256]
    sub = iota(0)

    def running(x):
        for shift in (1, 2, 4):
            x = x + jnp.where(sub >= shift, below(x, shift), 0.0)
        return x

    def octet(o, carry):
        def put_tangent(d, i, value):
            tangent[8 * i : 8 * i + 8, d * LANES : (d + 1) * LANES] = value

        gather(AROUND, around, o, both(ext_u), put_tangent, True)
        for half in range(2):

            def put_cells(d, i, value):
                cells[8 * i : 8 * i + 8, d * LANES : (d + 1) * LANES] = value

            gather(PAIR, pair, o * 2 + half, both(ext_h), put_cells, False)
            for q in range(4):
                group = o * 8 + half * 4 + q
                at = lanes_at(group)
                left, right = slice(q * LANES, (q + 1) * LANES), slice((q + 4) * LANES, (q + 5) * LANES)
                step = [cells[rows, right] - cells[rows, left] for rows in (TOP, LOW)]
                mean = [0.5 * (cells[rows, right] + cells[rows, left]) for rows in (TOP, LOW)]
                column = [running(x) for x in step]
                column[1] = column[1] + jnp.broadcast_to(column[0][7:8], (8, LANES))
                pressure = [gravity * (c - 0.5 * x) for c, x in zip(column, step)]
                u = [u_own[rows, at] for rows in (TOP, LOW)]
                upper = [
                    jnp.where(sub == 0, u[0], below(u[0], 1)),
                    jnp.where(sub == 0, jnp.broadcast_to(u[0][7:8], (8, LANES)), below(u[1], 1)),
                ]
                lower = [
                    jnp.where(sub == 7, jnp.broadcast_to(u[1][0:1], (8, LANES)), below(u[0], 7)),
                    jnp.where(sub == 7, u[1], below(u[1], 7)),
                ]
                own = [spread_row(ref, pl.ds(group, 1), slice(None)) for ref in (spacing, length, coriolis)]
                here = slice((half * 4 + q) * LANES, (half * 4 + q + 1) * LANES)
                for i, rows in enumerate((TOP, LOW)):
                    mix = mixing * (upper[i] + lower[i] - 2.0 * u[i])
                    slope = -pressure[i] / own[0] + own[2] * tangent[rows, here] + mix
                    fresh = velocity[rows, at] + tau * slope
                    u_next[rows, at] = fresh
                    flux[rows, at] = fresh * mean[i] * own[1]
        return carry

    lax.fori_loop(0, 6, octet, 0)
    sources = both(flux) if last else both(flux, u_next)
    width = 512 if last else 1024
    for o in range(2):

        def put_send(d, i, value):
            j, q = (o * 8 + d) // 4, (o * 8 + d) % 4
            at = j * width + (i // 2) * 512 + q * LANES
            out[8 * (i % 2) : 8 * (i % 2) + 8, at : at + LANES] = value

        gather(SEND_E, send_e, o, sources, put_send, False)


def cell_kernel(tau, last, place, *refs):
    thickness, flux, halo, area = refs[:4]
    side, refs = refs[4:10], refs[10:]
    if last:
        h_next, ext = refs
    else:
        send_c, (h_next, out, ext) = refs[:4], refs[4:]
    ext[:, : 48 * LANES] = flux[...]
    for j in range(4):
        ext[:, 48 * LANES + 512 * j : 48 * LANES + 512 * (j + 1)] = halo[:, j * place : j * place + 512]
    for o in range(2):

        def put(d, i, value):
            group = o * 8 + d
            rows, at = (TOP, LOW)[i], slice(group * LANES, (group + 1) * LANES)
            own = spread_row(area, pl.ds(group, 1), slice(None))
            h_next[rows, at] = thickness[rows, at] - tau * value / own

        gather(SIDE, side, o, both(ext), put, True)
    if not last:

        def put_h(d, i, value):
            out[8 * i : 8 * i + 8, d * LANES : (d + 1) * LANES] = value

        gather(SEND_C, send_c, 0, both(h_next), put_h, False)


def exchange_kernel(width, src, dst, send_sem, recv_sem):
    me = lax.axis_index("dom")
    count = lax.axis_size("dom")
    barrier = pltpu.get_barrier_semaphore()
    for offset in OFFSETS:
        peer = me + offset

        @pl.when((peer >= 0) & (peer < count))
        def _():
            pl.semaphore_signal(barrier, inc=1, device_id=(peer,), device_id_type=pl.DeviceIdType.MESH)

    pl.semaphore_wait(barrier, jnp.minimum(me, 2) + jnp.minimum(count - 1 - me, 2))

    def copy(place, peer):
        at = slice(place * width, (place + 1) * width)
        return pltpu.make_async_remote_copy(
            src_ref=src.at[:, at],
            dst_ref=dst.at[:, at],
            send_sem=send_sem.at[place],
            recv_sem=recv_sem.at[place],
            device_id=(peer,),
            device_id_type=pl.DeviceIdType.MESH,
        )

    for place, offset in enumerate(OFFSETS):
        peer, origin = me + offset, me - offset

        @pl.when((peer >= 0) & (peer < count))
        def _():
            copy(place, peer).start()

        @pl.when((origin < 0) | (origin >= count))
        def _():
            dst[:, place * width : (place + 1) * width] = jnp.zeros((16, width), jnp.float32)

    for place, offset in enumerate(OFFSETS):
        peer, origin = me + offset, me - offset

        @pl.when((peer >= 0) & (peer < count))
        def _():
            copy(place, peer).wait_send()

        @pl.when((origin >= 0) & (origin < count))
        def _():
            copy(place, origin).wait_recv()


def floats(*shape):
    return jax.ShapeDtypeStruct(shape, jnp.float32)


def whole(count):
    return [pl.BlockSpec(memory_space=VMEM)] * count


def local(kernel, name, args, in_specs, outs, out_specs, scratch):
    return pl.pallas_call(
        kernel,
        name=name,
        in_specs=in_specs,
        out_shape=outs,
        out_specs=out_specs,
        scratch_shapes=scratch,
        compiler_params=pltpu.CompilerParams(vmem_limit_bytes=48 << 20),
    )(*args)


def exchange(buffer):
    columns = buffer.shape[1]
    width = columns // 4
    return pl.pallas_call(
        functools.partial(exchange_kernel, width),
        name="exchange_halo",
        in_specs=whole(1),
        out_shape=floats(16, columns),
        out_specs=pl.BlockSpec(memory_space=VMEM),
        scratch_shapes=[pltpu.SemaphoreType.DMA((4,)), pltpu.SemaphoreType.DMA((4,))],
        compiler_params=pltpu.CompilerParams(collective_id=width // 256, has_side_effects=True),
    )(buffer)


def table_scratch(terms):
    return [VMEM((terms, 8, LANES), jnp.int32), VMEM((terms, 8, LANES), jnp.int32)]


def shards(
    thickness,
    velocity,
    send_cells,
    send_edges,
    cell_edges,
    cell_orient,
    edge_cells,
    edge_edges,
    edge_weights,
    cell_area,
    edge_spacing,
    edge_length,
    coriolis,
):
    made = local(
        sends_kernel,
        "plan_sends",
        (thickness, velocity, send_cells, send_edges),
        whole(4),
        SEND_E.shapes() + SEND_C.shapes() + [floats(16, 4 * 768)],
        SEND_E.out_specs() + SEND_C.out_specs() + whole(1),
        table_scratch(1) + [SMEM((8, LANES), jnp.int32), SMEM((8, LANES), jnp.int32)],
    )
    send_e, send_c, buffer = made[:4], made[4:8], made[8]
    made = local(
        plans_kernel,
        "plan_gathers",
        (edge_edges, edge_weights, edge_cells, cell_edges, cell_orient),
        whole(5),
        AROUND.shapes() + PAIR.shapes() + SIDE.shapes(),
        AROUND.out_specs() + PAIR.out_specs() + SIDE.out_specs(),
        table_scratch(10),
    )
    around, pair, side = made[:6], made[6:10], made[10:]
    halo_u = halo_h = exchange(buffer)
    u_place, h_place = (768, 0), (768, 512)
    h, u = thickness, velocity
    edge_coefs = [x.reshape(48, LANES) for x in (edge_spacing, edge_length, coriolis)]
    area = cell_area.reshape(16, LANES)
    for section in range(3):
        tau = time_step / (3 - section)
        last = section == 2
        width = 512 if last else 1024
        u, flux, buffer = local(
            functools.partial(edge_kernel, tau, last, u_place, h_place),
            "edge_section",
            (velocity, u, h, halo_u, halo_h, *edge_coefs, *around, *pair, *send_e),
            whole(8) + AROUND.in_specs() + PAIR.in_specs() + SEND_E.in_specs(),
            [floats(16, 48 * LANES), floats(16, 48 * LANES), floats(16, 4 * width)],
            whole(3),
            [
                VMEM((16, 64 * LANES), jnp.float32),
                VMEM((16, 24 * LANES), jnp.float32),
                VMEM((16, 8 * LANES), jnp.float32),
                VMEM((16, 8 * LANES), jnp.float32),
            ],
        )
        halo_u = exchange(buffer)
        u_place = (1024, 512)
        made = local(
            functools.partial(cell_kernel, tau, last, width),
            "cell_section",
            (thickness, flux, halo_u, area, *side) + (() if last else tuple(send_c)),
            whole(4) + SIDE.in_specs() + ([] if last else SEND_C.in_specs()),
            [floats(16, 16 * LANES)] + ([] if last else [floats(16, 8 * LANES)]),
            whole(1 if last else 2),
            [VMEM((16, 64 * LANES), jnp.float32)],
        )
        h = made[0]
        if not last:
            halo_h = exchange(made[1])
            h_place = (256, 0)
    return h, u


def solution(mesh):
    return jax.shard_map(
        shards,
        mesh=mesh,
        in_specs=(
            P(None, "dom"),
            P(None, "dom"),
            P("dom", None),
            P("dom", None),
            P(None, "dom"),
            P(None, "dom"),
            P(None, "dom"),
            P(None, "dom"),
            P(None, "dom"),
            P("dom"),
            P("dom"),
            P("dom"),
            P("dom"),
        ),
        out_specs=(P(None, "dom"), P(None, "dom")),
        check_vma=False,
    )
```

time: 1530 us -> 384 us (0.25)
  local copies, waits for them, and re-layouts: 1100 us -> 78.4 us
  Pallas kernels: 0 us -> 302 us
  other arithmetic: 249 us -> 0 us
  starting transfers between devices: 142 us -> 0 us
  waiting for transfers between devices: 21.2 us -> 0 us
    gather x27 -> x0, local copies, waits for them, and re-layouts: 953 us -> none  [the longest x3 633 us: shards(): jnp.take(ext_u, around_index, axis=0).reshape(-1, edge_count, levels)]
    pallas_call x0 -> x14, Pallas kernels: none -> 302 us  [the longest x8 237 us: local(): pl.pallas_call(kernel, name=name, in_specs=in_specs, out_shape=outs, out_...]
    select_n x16 -> x0, other arithmetic: 160 us -> none  [the longest x3 103 us: shards(): jnp.take(ext_u, around_index, axis=0).reshape(-1, edge_count, levels)]
    ppermute x36 -> x0, starting transfers between devices: 142 us -> none  [shifted(): return lax.ppermute(block, axis, route)]
    reduce_sum x6 -> x0, other arithmetic: 72 us -> none  [the longest x3 37.9 us: shards(): spread = jnp.sum(sides * signs[:, :, None], axis=1)]
    unnamed x170 -> x228, local copies, waits for them, and re-layouts: 45.7 us -> 78.4 us
    reshape x5 -> x0, local copies, waits for them, and re-layouts: 27.3 us -> none  [the longest x3 25.6 us: shards(): sides = jnp.take(ext_f, side_index, axis=0).reshape(cell_count, -1, levels)]
    concatenate x18 -> x0, local copies, waits for them, and re-layouts: 24.9 us -> none  [the longest x6 12.6 us: shards(): ext_f = jnp.concatenate([flux, halo_f], axis=0)]
  transfers between devices with their start and end apart: 36 -> 0, of which waited for: 7 -> 0; matrix products, arithmetic and copies ran while one was open for 51% -> 0% of each run, Pallas kernels for 0% -> 0%
where the time goes in v1:
time: 384 us; the launch traced here: 381 us
  Pallas kernels  302 us (79%)
  local copies, waits for them, and re-layouts  78.4 us (20%)
    pallas_call x8, Pallas kernels, local(): pl.pallas_call(kernel, name=name, in_specs=in_specs, out_shape=outs, out_...  237 us
    unnamed x228, local copies, waits for them, and re-layouts  78.4 us
    pallas_call x6, Pallas kernels, exchange(): pl.pallas_call(functools.partial(exchange_kernel, width), name='exchange_...  65 us

profile of v1, /device:TPU:9, one launch (start us, length us, event | category | flops | bytes accessed | tf_op | source)
XLA Modules:
  0.0 381.0 jit_solution(9962745457871325203)
XLA Ops:
  0.6 1.0 copy-done
  3.9 8.0 %plan_sends.1 = (s32[1,16,128]{2,1,0:T(8,128)S(1)}, s32[256,128]{1,0:T(8,128)S(1)}, s32[8,128]{1,0:T(8,128)S(1)}, s32[2]{0:T(128)S(1)}, s32[1,8,128]{2,1,0:T(8,1...) custom-call(f32[16,2048]{1,0:T(8,128)S(1)} %copy-done.2, ...), custom_call_target="tpu_custom_call" | custom-call | tf_op jit(solution)/shard_map/plan_sends/pallas_call | solution.py:408
  16.7 10.7 %exchange_halo.6.refs_3_.refs_4_ = f32[16,3072]{1,0:T(8,128)} custom-call(f32[16,3072]{1,0:T(8,128)} %copy-done.62), custom_call_target="tpu_custom_call" | custom-call | tf_op jit(solution)/shard_map/exchange_halo/pallas_call | solution.py:422
  27.4 1.0 copy-done.40
  28.4 1.0 copy-done.41
  31.9 42.3 %plan_gathers.1 = (s32[10,48,128]{2,1,0:T(8,128)S(1)}, s32[2304,128]{1,0:T(8,128)S(1)}, s32[72,128]{1,0:T(8,128)S(1)}, s32[6]{0:T(128)S(1)}, f32[10,48,128]{2,1,...) custom-call(s32[10,6144]{1,0:T(8,128)S(1)} %copy-done.40, ...), custom_call_target="tpu_custom_call" | custom-call | tf_op jit(solution)/shard_map/plan_gathers/pallas_call | solution.py:408
  76.2 1.1 copy-done.22
  81.7 51.5 %edge_section.3 = (f32[16,6144]{1,0:T(8,128)S(1)}, f32[16,6144]{1,0:T(8,128)S(1)}, f32[16,4096]{1,0:T(8,128)S(1)}) custom-call(f32[16,6144]{1,0:T(8,128)S(1)} %copy-done.1, f32[16,6144]{1,0:T(8,128)S(1)} %copy-done.1, f32[16,2048]{1,0:T(8,128)S(1)} %copy-done.3, f32[16,3072]{1,0:T(8,128)S(1)} %copy-done.22, f32[16,3072]{1,0:T(8,128)S(1)} %copy-done.22, ...), custom_call_target="tpu_custom_call" | custom-call | tf_op jit(solution)/shard_map/edge_section/pallas_call | solution.py:408
  135.5 13.0 %exchange_halo.7.refs_2_.refs_3_ = f32[16,4096]{1,0:T(8,128)} custom-call(f32[16,4096]{1,0:T(8,128)} %copy-done.54), custom_call_target="tpu_custom_call" | custom-call | tf_op jit(solution)/shard_map/exchange_halo/pallas_call | solution.py:422
  148.5 1.0 copy-done.5
  149.5 1.0 copy-done.9
  150.4 0.9 copy-done.14
  153.0 1.0 copy-done.47
  157.4 10.7 %cell_section.3 = (f32[16,2048]{1,0:T(8,128)S(1)}, f32[16,1024]{1,0:T(8,128)S(1)}) custom-call(f32[16,2048]{1,0:T(8,128)S(1)} %copy-done.3, f32[16,6144]{1,0:T(8,128)S(1)} %copy-done.47, f32[16,4096]{1,0:T(8,128)S(1)} %copy-done.14, f32[16,128]{1,0:T(8,128)S(1)} %bitcast.13, s32[6,16,128]{2,1,0:T(8,128)S(1)} %copy-done.29, s32[640,128]{1,0:T(8,128)S(1)} %copy-done.5, ...), custom_call_target="tpu_custom_call" | custom-call | tf_op jit(solution)/shard_map/cell_section/pallas_call | solution.py:408
  169.4 9.0 %exchange_halo.8.refs_4_ = f32[16,1024]{1,0:T(8,128)} custom-call(f32[16,1024]{1,0:T(8,128)} %copy-done.84), custom_call_target="tpu_custom_call" | custom-call | tf_op jit(solution)/shard_map/exchange_halo/pallas_call | solution.py:422
  179.3 0.9 copy-done.17
  182.1 1.0 copy-done.39
  191.1 51.5 %edge_section.4 = (f32[16,6144]{1,0:T(8,128)S(1)}, f32[16,6144]{1,0:T(8,128)S(1)}, f32[16,4096]{1,0:T(8,128)S(1)}) custom-call(f32[16,6144]{1,0:T(8,128)S(1)} %copy-done.1, f32[16,6144]{1,0:T(8,128)S(1)} %copy-done.39, f32[16,2048]{1,0:T(8,128)S(1)} %copy-done.69, f32[16,4096]{1,0:T(8,128)S(1)} %copy-done.15, f32[16,1024]{1,0:T(8,128)S(1)} %copy-done.52, ...), custom_call_target="tpu_custom_call" | custom-call | tf_op jit(solution)/shard_map/edge_section/pallas_call | solution.py:408
  244.8 12.3 %exchange_halo.9.refs_2_.refs_3_ = f32[16,4096]{1,0:T(8,128)} custom-call(f32[16,4096]{1,0:T(8,128)} %copy-done.53), custom_call_target="tpu_custom_call" | custom-call | tf_op jit(solution)/shard_map/exchange_halo/pallas_call | solution.py:422
  257.1 1.0 copy-done.6
  258.0 1.0 copy-done.10
  259.0 0.9 copy-done.12
  261.6 1.0 copy-done.45
  266.0 10.9 %cell_section.4 = (f32[16,2048]{1,0:T(8,128)S(1)}, f32[16,1024]{1,0:T(8,128)S(1)}) custom-call(f32[16,2048]{1,0:T(8,128)S(1)} %copy-done.3, f32[16,6144]{1,0:T(8,128)S(1)} %copy-done.45, f32[16,4096]{1,0:T(8,128)S(1)} %copy-done.12, f32[16,128]{1,0:T(8,128)S(1)} %bitcast.14, s32[6,16,128]{2,1,0:T(8,128)S(1)} %copy-done.30, s32[640,128]{1,0:T(8,128)S(1)} %copy-done.6, ...), custom_call_target="tpu_custom_call" | custom-call | tf_op jit(solution)/shard_map/cell_section/pallas_call | solution.py:408
  278.2 9.0 %exchange_halo.10.refs_4_ = f32[16,1024]{1,0:T(8,128)} custom-call(f32[16,1024]{1,0:T(8,128)} %copy-done.83), custom_call_target="tpu_custom_call" | custom-call | tf_op jit(solution)/shard_map/exchange_halo/pallas_call | solution.py:422
  290.9 1.0 copy-done.37
  299.9 52.0 %edge_section.5 = (f32[16,6144]{1,0:T(8,128)}, f32[16,6144]{1,0:T(8,128)S(1)}, f32[16,2048]{1,0:T(8,128)S(1)}) custom-call(f32[16,6144]{1,0:T(8,128)S(1)} %copy-done.1, f32[16,6144]{1,0:T(8,128)S(1)} %copy-done.37, f32[16,2048]{1,0:T(8,128)S(1)} %copy-done.67, f32[16,4096]{1,0:T(8,128)S(1)} %copy-done.13, f32[16,1024]{1,0:T(8,128)S(1)} %copy-done.51, ...), custom_call_target="tpu_custom_call" | custom-call | tf_op jit(solution)/shard_map/edge_section/pallas_call | solution.py:408
  353.3 11.2 %exchange_halo.11.refs_2_ = f32[16,2048]{1,0:T(8,128)} custom-call(f32[16,2048]{1,0:T(8,128)} %copy-done.73), custom_call_target="tpu_custom_call" | custom-call | tf_op jit(solution)/shard_map/exchange_halo/pallas_call | solution.py:422
  364.5 1.0 copy-done.7
  365.5 1.0 copy-done.11
  368.9 1.0 copy-done.43
  371.3 9.8 %cell_section.5 = f32[16,2048]{1,0:T(8,128)} custom-call(f32[16,2048]{1,0:T(8,128)S(1)} %copy-done.3, f32[16,6144]{1,0:T(8,128)S(1)} %copy-done.43, f32[16,2048]{1,0:T(8,128)S(1)} %copy-done.27, f32[16,128]{1,0:T(8,128)S(1)} %bitcast.15, s32[6,16,128]{2,1,0:T(8,128)S(1)} %copy-done.31, s32[640,128]{1,0:T(8,128)S(1)} %copy-done.7, s32[24,128]{1,0:T(8,128)S(1)} %copy-done.77, ...), custom_call_target="tpu_custom_call" | custom-call | tf_op jit(solution)/shard_map/cell_section/pallas_call | solution.py:408
  (210 shorter events, 60.7 us)
Async XLA Ops:
  0.6 1.0 copy-start
  3.9 72.2 %copy-start.1 = (f32[16,6144]{1,0:T(8,128)S(1)}, f32[16,6144]{1,0:T(8,128)}, u32[]{:S(2)}) copy-start(f32[16,6144]{1,0:T(8,128)} %refs_0_.10) | copy-start | bytes 1179652
  3.9 72.2 %copy-start.3 = (f32[16,2048]{1,0:T(8,128)S(1)}, f32[16,2048]{1,0:T(8,128)}, u32[]{:S(2)}) copy-start(f32[16,2048]{1,0:T(8,128)} %refs_0_.11) | copy-start | bytes 393220
  3.9 72.2 %copy-start.55 = (f32[6144]{0:T(1024)S(1)}, f32[6144]{0:T(1024)}, u32[]{:S(2)}) copy-start(f32[6144]{0:T(1024)} %param.23) | copy-start | bytes 73732
  27.4 1.0 copy-start.40
  28.4 1.0 copy-start.41
  76.1 57.1 %copy-start.8 = (f32[640,128]{1,0:T(8,128)}, f32[640,128]{1,0:T(8,128)S(1)}, u32[]{:S(2)}) copy-start(f32[640,128]{1,0:T(8,128)S(1)} %get-tuple-element.63.refs_9_) | copy-start | bytes 983044
  76.1 57.1 %copy-start.16 = (s32[10,48,128]{2,1,0:T(8,128)}, s32[10,48,128]{2,1,0:T(8,128)S(1)}, u32[]{:S(2)}) copy-start(s32[10,48,128]{2,1,0:T(8,128)S(1)} %get-tuple-element.41.refs_8_) | copy-start | bytes 737284
  76.1 57.1 %copy-start.19 = (f32[10,48,128]{2,1,0:T(8,128)}, f32[10,48,128]{2,1,0:T(8,128)S(1)}, u32[]{:S(2)}) copy-start(f32[10,48,128]{2,1,0:T(8,128)S(1)} %get-tuple-element.45.refs_12_) | copy-start | bytes 737284
  76.1 57.1 %copy-start.32 = (f32[6,16,128]{2,1,0:T(8,128)}, f32[6,16,128]{2,1,0:T(8,128)S(1)}, u32[]{:S(2)}) copy-start(f32[6,16,128]{2,1,0:T(8,128)S(1)} %get-tuple-element.62.refs_8_) | copy-start | bytes 147460
  76.1 57.1 %copy-start.48 = (s32[72,128]{1,0:T(8,128)}, s32[72,128]{1,0:T(8,128)S(1)}, u32[]{:S(2)}) copy-start(s32[72,128]{1,0:T(8,128)S(1)} %get-tuple-element.43.refs_10_) | copy-start | bytes 110596
  76.1 57.1 %copy-start.63 = (s32[40,128]{1,0:T(8,128)}, s32[40,128]{1,0:T(8,128)S(1)}, u32[]{:S(2)}) copy-start(s32[40,128]{1,0:T(8,128)S(1)} %get-tuple-element.49.refs_16_) | copy-start | bytes 61444
  76.1 57.1 %copy-start.99 = (s32[2]{0:T(128)}, s32[2]{0:T(128)S(1)}, u32[]{:S(2)}) copy-start(s32[2]{0:T(128)S(1)} %get-tuple-element.61.refs_7_) | copy-start | bytes 28
  76.1 57.1 %copy-start.107 = (s32[6]{0:T(128)}, s32[6]{0:T(128)S(1)}, u32[]{:S(2)}) copy-start(s32[6]{0:T(128)S(1)} %get-tuple-element.44.refs_11_) | copy-start | bytes 76
  76.1 57.1 %copy-start.110 = (s32[12]{0:T(128)}, s32[12]{0:T(128)S(1)}, u32[]{:S(2)}) copy-start(s32[12]{0:T(128)S(1)} %get-tuple-element.50.refs_17_) | copy-start | bytes 148
  76.2 1.2 copy-start.22
  81.7 66.8 %copy-start.78 = (f32[2048]{0:T(1024)S(1)}, f32[2048]{0:T(1024)}, u32[]{:S(2)}) copy-start(f32[2048]{0:T(1024)} %param.22) | copy-start | bytes 24580
  148.5 1.0 copy-start.5
  149.5 1.0 copy-start.9
  150.4 0.9 copy-start.14
  153.0 1.0 copy-start.47
  178.4 1.0 copy-start.15
  182.1 1.0 copy-start.39
  257.1 1.0 copy-start.6
  258.0 1.0 copy-start.10
  259.0 0.9 copy-start.12
  261.6 1.0 copy-start.45
  287.1 1.0 copy-start.13
  290.9 1.0 copy-start.37
  364.5 1.0 copy-start.7
  365.5 1.0 copy-start.11
  368.9 1.0 copy-start.43
  (82 other events, 59.7 us)

commit v2 on v0

--- a/solution.py
+++ b/solution.py
@@ -1,11 +1,444 @@
+import functools
+
 import jax
 import jax.numpy as jnp
 from jax import lax
+from jax.experimental import pallas as pl
+from jax.experimental.pallas import tpu as pltpu
 from jax.sharding import PartitionSpec as P
 
 gravity = 0.1
 mixing = 0.2
 time_step = 0.5
+LANES = 128
+OFFSETS = (-2, -1, 1, 2)
+VMEM = pltpu.VMEM
+SMEM = pltpu.SMEM
+TOP, LOW = slice(0, 8), slice(8, 16)
+
+
+class Plan:
+    rows = weights = ids = 0
+
+    def __init__(self, terms, octets, first, chunks, cap, turns, cuts, weighted):
+        self.terms, self.octets, self.first, self.chunks = terms, octets, first, chunks
+        self.cap, self.turns, self.cuts, self.weighted = cap, turns, cuts, weighted
+        self.row_at, self.weight_at, self.id_at = Plan.rows, Plan.weights, Plan.ids
+        self.id_rows = -(-cap // LANES)
+        Plan.rows += octets * cap
+        Plan.weights += octets * cap * weighted
+        Plan.ids += octets * self.id_rows
+
+
+AROUND = Plan(10, 6, 0, 48, 272, 4, 2, True), Plan(10, 6, 48, 16, 104, 2, 1, True)
+PAIR = Plan(1, 12, 0, 16, 56, 1, 1, False), Plan(1, 12, 16, 8, 32, 1, 1, False)
+SIDE = Plan(6, 2, 0, 48, 208, 4, 2, True), Plan(6, 2, 48, 16, 80, 2, 1, True)
+SEND_E = Plan(1, 2, 0, 48, 112, 2, 1, False)
+SEND_C = Plan(1, 1, 0, 16, 64, 1, 1, False)
+ROWS, WEIGHTS, IDS = Plan.rows, Plan.weights, -(-Plan.ids // 8) * 8
+
+
+def iota(axis):
+    return lax.broadcasted_iota(jnp.int32, (8, LANES), axis)
+
+
+def spread(row):
+    return jnp.broadcast_to(row, (8, LANES))
+
+
+def turn(x, shift):
+    return pltpu.roll(x, shift, 0)
+
+
+def lanes_at(position):
+    return pl.ds(pl.multiple_of(position * LANES, LANES), LANES)
+
+
+def sums_of_rows(parts, sub):
+    for bit in (1, 2, 4):
+        first = (sub & bit) == 0
+        parts = [jnp.where(first, a, b) + turn(jnp.where(first, b, a), bit) for a, b in zip(parts[::2], parts[1::2])]
+    return parts[0]
+
+
+def build(plan, raw, scale, packed, weights, ids, over, chunks, keys, loads):
+    sub, lane = iota(0), iota(1)
+    tiles = -(-plan.chunks // 8)
+    numbers = [sub + 8 * v for v in range(tiles)]
+
+    def octet(o, carry):
+        at = pl.ds(pl.multiple_of(o * 8, 8), 8)
+        for k in range(plan.terms):
+            chunks[k] = lax.shift_right_logical(raw[k, at, :], 7) - plan.first
+
+        def rank(k, counts):
+            counts = list(counts)
+            parts = []
+            for s in range(8):
+                chunk = spread(chunks[k, s : s + 1, :])
+                part = None
+                for v in range(tiles):
+                    hit = chunk == numbers[v]
+                    seen = jnp.where(hit, counts[v], 0)
+                    part = seen if part is None else part + seen
+                    counts[v] = jnp.where(hit, counts[v] + 1, counts[v])
+                parts.append(part)
+            keys[k] = sums_of_rows(parts, sub)
+            return tuple(counts)
+
+        counts = lax.fori_loop(0, plan.terms, rank, tuple(jnp.zeros((8, LANES), jnp.int32) for _ in range(tiles)))
+        most = [spread(jnp.max(c, axis=1, keepdims=True)) for c in counts]
+        upto = most
+        for shift in (1, 2, 4):
+            upto = [x + jnp.where(sub >= shift, turn(x, shift), 0) for x in upto]
+        before = jnp.zeros((8, LANES), jnp.int32)
+        starts = jnp.zeros((8, LANES), jnp.int32)
+        for v in range(tiles):
+            starts = starts + jnp.where(lane == numbers[v], upto[v] - most[v] + before, 0)
+            before = before + spread(upto[v][7:8])
+        for shift in (1, 2, 4):
+            starts = starts + turn(starts, shift)
+        over[...] = jnp.maximum(over[...], jnp.where(before > plan.cap, 1.0, 0.0))
+        for k in range(plan.terms):
+            chunk = chunks[k]
+            inside = (chunk >= 0) & (chunk < plan.chunks)
+            start = jnp.take_along_axis(starts, chunk & 127, axis=1, mode="promise_in_bounds")
+            keys[k] = jnp.where(inside, start + keys[k], -1)
+            loads[k] = (raw[k, at, :] & 127) | (sub << 7) | (jnp.where(inside, chunk, 0) << 11)
+        places = [jnp.zeros((8, LANES), jnp.int32) for _ in range(plan.id_rows)]
+        size = plan.cap // 8 // plan.cuts
+        for cut in range(plan.cuts):
+            tops = [8 * (cut * size + v) for v in range(size)]
+
+            def match(k, found):
+                load, weight = list(found[:size]), list(found[size:])
+                for s in range(8):
+                    wanted = spread(keys[k, s : s + 1, :])
+                    value = spread(loads[k, s : s + 1, :])
+                    if plan.weighted:
+                        factor = spread(scale[k, pl.ds(o * 8 + s, 1), :])
+                    for v in range(size):
+                        here = wanted == sub + tops[v]
+                        load[v] = jnp.where(here, value, load[v])
+                        if plan.weighted:
+                            weight[v] = jnp.where(here, factor, weight[v])
+                return (*load, *weight)
+
+            begin = [jnp.full((8, LANES), 8 << 7, jnp.int32)] * size
+            begin += [jnp.zeros((8, LANES), jnp.float32)] * (size * plan.weighted)
+            found = lax.fori_loop(0, plan.terms, match, tuple(begin))
+            for v in range(size):
+                load = found[v]
+                offset = o * plan.cap + tops[v]
+                packed[pl.ds(pl.multiple_of(plan.row_at + offset, 8), 8), :] = load & 2047
+                if plan.weighted:
+                    weights[pl.ds(pl.multiple_of(plan.weight_at + offset, 8), 8), :] = found[size + v]
+                own = jnp.max(load >> 11, axis=1, keepdims=True)
+                which = tops[v] // LANES
+                places[which] = places[which] + jnp.where(lane == sub + tops[v] % LANES, own, 0)
+        for i, place in enumerate(places):
+            ids[pl.ds(plan.id_at + o * plan.id_rows + i, 1), :] = jnp.sum(place, axis=0, keepdims=True)
+        return carry
+
+    lax.fori_loop(0, plan.octets, octet, 0)
+
+
+def plans_kernel(send_c, send_e, cell_edges, cell_orient, edge_cells, edge_edges, edge_weights, *rest):
+    packed, weights, ids, over, around, factors, pair, side, signs, to_e, to_c, chunks, keys, loads = rest
+    over[...] = jnp.zeros((8, LANES), jnp.float32)
+    ids[...] = jnp.zeros((IDS, LANES), jnp.int32)
+    for j in range(4):
+        for q in range(4):
+            to_e[0, 4 * j + q : 4 * j + q + 1, :] = send_e[j : j + 1, q * LANES : (q + 1) * LANES]
+        for q in range(2):
+            to_c[0, 2 * j + q : 2 * j + q + 1, :] = send_c[j : j + 1, q * LANES : (q + 1) * LANES]
+    for g in range(48):
+        at = slice(g * LANES, (g + 1) * LANES)
+        for k in range(10):
+            around[k, g : g + 1, :] = edge_edges[k : k + 1, at]
+            factors[k, g : g + 1, :] = edge_weights[k : k + 1, at]
+        for k in range(2):
+            to = g // 4 * 8 + k * 4 + g % 4
+            pair[0, to : to + 1, :] = edge_cells[k : k + 1, at]
+    for g in range(16):
+        at = slice(g * LANES, (g + 1) * LANES)
+        for k in range(6):
+            side[k, g : g + 1, :] = cell_edges[k : k + 1, at]
+            signs[k, g : g + 1, :] = (2 * cell_orient[k : k + 1, at] - 1).astype(jnp.float32)
+    tail = (packed, weights, ids, over, chunks, keys, loads)
+    build(SEND_E, to_e, None, *tail)
+    build(SEND_C, to_c, None, *tail)
+    for i in range(2):
+        build(AROUND[i], around, factors, *tail)
+        build(PAIR[i], pair, None, *tail)
+        build(SIDE[i], side, signs, *tail)
+
+
+def gather(plan, lists, o, sources, sums):
+    packed, weights, ids = lists
+    steps = plan.cap // plan.turns
+
+    def step(t, sums):
+        sums = list(sums)
+        for r in range(steps):
+            row = t * steps + r
+            at = o * plan.cap + row
+            chunk = ids[plan.id_at + o * plan.id_rows + row // LANES, row % LANES]
+            load = spread(packed[pl.ds(plan.row_at + at, 1), :])
+            pick, goal = load & 127, lax.shift_right_logical(load, 7)
+            found = [jnp.take_along_axis(take(chunk), pick, axis=1, mode="promise_in_bounds") for take in sources]
+            if plan.weighted:
+                factor = spread(weights[pl.ds(plan.weight_at + at, 1), :])
+                found = [value * factor for value in found]
+            for d in range(8):
+                mine = goal == d
+                for i, value in enumerate(found):
+                    j = d * len(sources) + i
+                    sums[j] = jnp.where(mine, sums[j] + value if plan.weighted else value, sums[j])
+        return tuple(sums)
+
+    return lax.fori_loop(0, plan.turns, step, tuple(sums))
+
+
+def zeros(count):
+    return [jnp.zeros((8, LANES), jnp.float32) for _ in range(count)]
+
+
+def both(*takes):
+    return [functools.partial(take, rows) for take in takes for rows in (TOP, LOW)]
+
+
+def table(ref):
+    return lambda rows, chunk: ref[chunk, rows, :]
+
+
+FIELDS = 3
+
+
+def step_kernel(thickness, velocity, packed_in, weights_in, spacing_in, length_in, coriolis_in, area_in, ids, *rest):
+    h_out, u_out = rest[:2]
+    (h0, u0, packed, weights, spacing, length, coriolis, area, loaded) = rest[2:11]
+    (h, u, flux, tangent, cells, spread_sum, send_h, send_u, send_f, halo_h, halo_u, halo_f, near, sent, came) = rest[11:]
+    me = lax.axis_index("dom")
+    count = lax.axis_size("dom")
+    barrier = pltpu.get_barrier_semaphore()
+    for offset in OFFSETS:
+        peer = me + offset
+
+        @pl.when((peer >= 0) & (peer < count))
+        def _():
+            pl.semaphore_signal(barrier, inc=1, device_id=(peer,), device_id_type=pl.DeviceIdType.MESH)
+
+    lists = (packed, weights, ids)
+    given = (thickness, velocity, packed_in, spacing_in, length_in, coriolis_in, area_in, weights_in)
+    kept = (h0, u0, packed, spacing, length, coriolis, area, weights)
+    copies = [pltpu.make_async_copy(a, b, loaded.at[i]) for i, (a, b) in enumerate(zip(given, kept))]
+    for copy in copies:
+        copy.start()
+    sends, halos = (send_h, send_u, send_f), (halo_h, halo_u, halo_f)
+    widths = (2, 4, 4)
+
+    def copy_of(field, k, place, peer):
+        at = pl.ds(place * widths[field], widths[field])
+        return pltpu.make_async_remote_copy(
+            src_ref=sends[field].at[k, at],
+            dst_ref=halos[field].at[k, at],
+            send_sem=sent.at[k, field, place],
+            recv_sem=came.at[k, field, place],
+            device_id=(peer,),
+            device_id_type=pl.DeviceIdType.MESH,
+        )
+
+    def start(field, k):
+        for place, offset in enumerate(OFFSETS):
+            peer = me + offset
+
+            @pl.when((peer >= 0) & (peer < count))
+            def _():
+                copy_of(field, k, place, peer).start()
+
+    def arrive(field, k):
+        for place, offset in enumerate(OFFSETS):
+            origin = me - offset
+
+            @pl.when((origin >= 0) & (origin < count))
+            def _():
+                copy_of(field, k, place, origin).wait_recv()
+
+        near[: 4 * widths[field]] = halos[field][k]
+
+    for place, offset in enumerate(OFFSETS):
+        origin = me - offset
+
+        @pl.when((origin < 0) | (origin >= count))
+        def _():
+            for halo, width in zip(halos, widths):
+                for k in range(3):
+                    halo[k, place * width : (place + 1) * width] = jnp.zeros((width, 16, LANES), jnp.float32)
+
+    def send_edges(k, *refs):
+        sources = both(*(table(source) for source, _ in refs))
+
+        def octet(o, carry):
+            found = gather(SEND_E, lists, o, sources, zeros(8 * len(sources)))
+            for d in range(8):
+                for i, (_, buffer) in enumerate(refs):
+                    for j, rows in enumerate((TOP, LOW)):
+                        buffer[k, o * 8 + d, rows, :] = found[d * len(sources) + 2 * i + j]
+            return carry
+
+        lax.fori_loop(0, 2, octet, 0)
+
+    def send_cells(k, source):
+        found = gather(SEND_C, lists, 0, both(table(source)), zeros(16))
+        for d in range(8):
+            for j, rows in enumerate((TOP, LOW)):
+                send_h[k, d, rows, :] = found[2 * d + j]
+
+    for i in range(3):
+        copies[i].wait()
+    for group in range(48):
+        u[group] = u0[:, group * LANES : (group + 1) * LANES]
+    for group in range(16):
+        h[group] = h0[:, group * LANES : (group + 1) * LANES]
+    send_edges(0, (u, send_u))
+    send_cells(0, h)
+    pl.semaphore_wait(barrier, jnp.minimum(me, 2) + jnp.minimum(count - 1 - me, 2))
+    start(0, 0)
+    start(1, 0)
+    for i in range(3, len(copies)):
+        copies[i].wait()
+    sub = iota(0)
+
+    def running(x):
+        for shift in (1, 2, 4):
+            x = x + jnp.where(sub >= shift, turn(x, shift), 0.0)
+        return x
+
+    def sweep(plan, take, ref, fresh):
+        def octet(o, carry):
+            at = [o * 8 + d for d in range(8)]
+            begin = zeros(16) if fresh else [ref[a, rows, :] for a in at for rows in (TOP, LOW)]
+            found = gather(plan, lists, o, both(take), begin)
+            for d in range(8):
+                for j, rows in enumerate((TOP, LOW)):
+                    ref[at[d], rows, :] = found[2 * d + j]
+            return carry
+
+        lax.fori_loop(0, plan.octets, octet, 0)
+
+    def edges_of(k, tau):
+        def quad(q, carry):
+            for e in range(4):
+                group = q * 4 + e
+                at = lanes_at(group)
+                left, right = q * 8 + e, q * 8 + 4 + e
+                step = [cells[right, rows, :] - cells[left, rows, :] for rows in (TOP, LOW)]
+                mean = [0.5 * (cells[right, rows, :] + cells[left, rows, :]) for rows in (TOP, LOW)]
+                column = [running(x) for x in step]
+                column[1] = column[1] + spread(column[0][7:8])
+                pressure = [gravity * (c - 0.5 * x) for c, x in zip(column, step)]
+                now = [u[group, rows, :] for rows in (TOP, LOW)]
+                upper = [
+                    jnp.where(sub == 0, now[0], turn(now[0], 1)),
+                    jnp.where(sub == 0, spread(now[0][7:8]), turn(now[1], 1)),
+                ]
+                lower = [
+                    jnp.where(sub == 7, spread(now[1][0:1]), turn(now[0], 7)),
+                    jnp.where(sub == 7, now[1], turn(now[1], 7)),
+                ]
+                gap, long, spin = [spread(ref[pl.ds(group, 1), :]) for ref in (spacing, length, coriolis)]
+                for i, rows in enumerate((TOP, LOW)):
+                    mix = mixing * (upper[i] + lower[i] - 2.0 * now[i])
+                    fresh = u0[rows, at] + tau * (-pressure[i] / gap + spin * tangent[group, rows, :] + mix)
+                    u[group, rows, :] = fresh
+                    flux[group, rows, :] = fresh * mean[i] * long
+            return carry
+
+        lax.fori_loop(0, 12, quad, 0)
+
+    def section(k, carry):
+        tau = time_step / (3 - k).astype(jnp.float32)
+        sweep(AROUND[0], table(u), tangent, True)
+        sweep(PAIR[0], table(h), cells, True)
+        arrive(1, k)
+        sweep(AROUND[1], table(near), tangent, False)
+        arrive(0, k)
+        sweep(PAIR[1], table(near), cells, False)
+        edges_of(k, tau)
+
+        later = jnp.minimum(k + 1, 2)
+
+        @pl.when(k < 2)
+        def _():
+            send_edges_pair(k, later)
+            start(2, k)
+            start(1, later)
+
+        @pl.when(k == 2)
+        def _():
+            send_edges(2, (flux, send_f))
+            start(2, 2)
+
+        sweep(SIDE[0], table(flux), spread_sum, True)
+        arrive(2, k)
+        sweep(SIDE[1], table(near), spread_sum, False)
+        for group in range(16):
+            at = slice(group * LANES, (group + 1) * LANES)
+            own = spread(area[group : group + 1, :])
+            for rows in (TOP, LOW):
+                h[group, rows, :] = h0[rows, at] - tau * spread_sum[group, rows, :] / own
+
+        @pl.when(k < 2)
+        def _():
+            send_cells(later, h)
+            start(0, later)
+
+        return carry
+
+    def send_edges_pair(k, later):
+        sources = both(table(flux), table(u))
+
+        def octet(o, carry):
+            found = gather(SEND_E, lists, o, sources, zeros(32))
+            for d in range(8):
+                at = o * 8 + d
+                for j, rows in enumerate((TOP, LOW)):
+                    send_f[k, at, rows, :] = found[4 * d + j]
+                    send_u[later, at, rows, :] = found[4 * d + 2 + j]
+            return carry
+
+        lax.fori_loop(0, 2, octet, 0)
+
+    lax.fori_loop(0, 3, section, 0)
+    for group in range(48):
+        u_out[:, group * LANES : (group + 1) * LANES] = u[group]
+    for group in range(16):
+        h_out[:, group * LANES : (group + 1) * LANES] = h[group]
+    for field in range(FIELDS):
+        for k in range(3):
+            for place, offset in enumerate(OFFSETS):
+                peer = me + offset
+
+                @pl.when((peer >= 0) & (peer < count))
+                def _():
+                    copy_of(field, k, place, peer).wait_send()
+
+
+def floats(*shape):
+    return jax.ShapeDtypeStruct(shape, jnp.float32)
+
+
+def ints(*shape):
+    return jax.ShapeDtypeStruct(shape, jnp.int32)
+
+
+def whole(count):
+    return [pl.BlockSpec(memory_space=VMEM)] * count
+
+
+def held(dtype, *shapes):
+    return [VMEM(shape, dtype) for shape in shapes]
 
 
 def shifted(block, axis, distance):
@@ -39,7 +472,7 @@
     return jnp.concatenate([arrived[offset] for offset in offsets], axis=0)
 
 
-def shards(
+def general(
     thickness,
     velocity,
     send_cells,
@@ -94,6 +527,61 @@
     return (rows_h.T, rows_u.T)
 
 
+def shards(
+    thickness,
+    velocity,
+    send_cells,
+    send_edges,
+    cell_edges,
+    cell_orient,
+    edge_cells,
+    edge_edges,
+    edge_weights,
+    cell_area,
+    edge_spacing,
+    edge_length,
+    coriolis,
+):
+    index = (send_cells, send_edges, cell_edges, cell_orient, edge_cells, edge_edges)
+    around, side = (10, 48, LANES), (6, 16, LANES)
+    packed, weights, ids, over = pl.pallas_call(
+        plans_kernel,
+        name="plan_gathers",
+        in_specs=whole(7),
+        out_shape=[ints(ROWS, LANES), floats(WEIGHTS, LANES), ints(IDS, LANES), floats(8, LANES)],
+        out_specs=whole(4),
+        scratch_shapes=held(jnp.int32, around)
+        + held(jnp.float32, around)
+        + held(jnp.int32, (1, 96, LANES), side)
+        + held(jnp.float32, side)
+        + held(jnp.int32, (1, 16, LANES), (1, 8, LANES), *[(10, 8, LANES)] * 3),
+        compiler_params=pltpu.CompilerParams(vmem_limit_bytes=24 << 20),
+    )(*index, edge_weights)
+    overs = lax.psum(over[:1], "dom")[0, 0]
+    coefs = [x.reshape(48, LANES) for x in (edge_spacing, edge_length, coriolis)] + [cell_area.reshape(16, LANES)]
+    rows, groups, halo = (48, LANES), (48, 16, LANES), (3, 16, 16, LANES)
+    fast = pl.pallas_call(
+        step_kernel,
+        name="three_sections",
+        in_specs=[pl.BlockSpec(memory_space=pl.ANY)] * 8 + [pl.BlockSpec(memory_space=SMEM)],
+        out_shape=[floats(16, 16 * LANES), floats(16, 48 * LANES)],
+        out_specs=whole(2),
+        scratch_shapes=held(jnp.float32, (16, 16 * LANES), (16, 48 * LANES))
+        + held(jnp.int32, (ROWS, LANES))
+        + held(jnp.float32, (WEIGHTS, LANES), rows, rows, rows, (16, LANES))
+        + [pltpu.SemaphoreType.DMA((8,))]
+        + held(jnp.float32, (16, 16, LANES), groups, groups, groups, (96, 16, LANES), (16, 16, LANES))
+        + held(jnp.float32, (3, 8, 16, LANES), halo, halo, (3, 8, 16, LANES), halo, halo, (16, 16, LANES))
+        + [pltpu.SemaphoreType.DMA((3, FIELDS, 4)), pltpu.SemaphoreType.DMA((3, FIELDS, 4))],
+        compiler_params=pltpu.CompilerParams(collective_id=0, has_side_effects=True, vmem_limit_bytes=32 << 20),
+    )(thickness, velocity, packed, weights, *coefs, ids)
+
+    def in_general():
+        return general(thickness, velocity, *index, edge_weights, cell_area, edge_spacing, edge_length, coriolis)
+
+    return lax.cond(overs > 0, in_general, lambda: tuple(fast))
+
+
 def solution(mesh):
     return jax.shard_map(
         shards,

time: 1530 us -> 238 us (0.16); the launches traced: 1510 us -> 238 us
  local copies, waits for them, and re-layouts: 1100 us -> 5.81 us
  other arithmetic: 249 us -> 0 us
  Pallas kernels: 0 us -> 165 us
  starting transfers between devices: 142 us -> 0 us
  blocking collectives: 0 us -> 66.4 us
  waiting for transfers between devices: 21.2 us -> 0 us
    gather x27 -> x0, local copies, waits for them, and re-layouts: 953 us -> none  [the longest x3 633 us: shards(): jnp.take(ext_u, around_index, axis=0).reshape(-1, edge_count, levels)]
    pallas_call x0 -> x2, Pallas kernels: none -> 165 us  [the longest x1 121 us: shards(): pl.pallas_call(step_kernel, name='three_sections', in_specs=[pl.BlockSpec...]
    select_n x16 -> x0, other arithmetic: 160 us -> none  [the longest x3 103 us: shards(): jnp.take(ext_u, around_index, axis=0).reshape(-1, edge_count, levels)]
    ppermute x36 -> x0, starting transfers between devices: 142 us -> none  [shifted(): return lax.ppermute(block, axis, route)]
    reduce_sum x6 -> x0, other arithmetic: 72 us -> none  [the longest x3 37.9 us: shards(): spread = jnp.sum(sides * signs[:, :, None], axis=1)]
    psum x0 -> x1, blocking collectives: none -> 66.4 us  [shards(): overs = lax.psum(over[:1], 'dom')[0, 0]]
    unnamed x170 -> x6, local copies, waits for them, and re-layouts: 45.7 us -> 5.81 us
    reshape x5 -> x0, local copies, waits for them, and re-layouts: 27.3 us -> none  [the longest x3 25.6 us: shards(): sides = jnp.take(ext_f, side_index, axis=0).reshape(cell_count, -1, levels)]
  transfers between devices with their start and end apart: 36 -> 0, of which waited for: 7 -> 0; matrix products, arithmetic and copies ran while one was open for 51% -> 0% of each run, Pallas kernels for 0% -> 0%
where the time goes in v2:
time: 238 us
  Pallas kernels  165 us (69%)
  blocking collectives  66.4 us (28%)
  local copies, waits for them, and re-layouts  5.81 us (2%)
    pallas_call x1, Pallas kernels, shards(): pl.pallas_call(step_kernel, name='three_sections', in_specs=[pl.BlockSpec...  121 us
    psum x1, blocking collectives, shards(): overs = lax.psum(over[:1], 'dom')[0, 0]  66.4 us
    pallas_call x1, Pallas kernels, shards(): pl.pallas_call(plans_kernel, name='plan_gathers', in_specs=whole(7), out_...  43.5 us
    unnamed x6, local copies, waits for them, and re-layouts  5.81 us

profile of v2, /device:TPU:9, one launch (start us, length us, event | category | flops | bytes accessed | tf_op | source)
XLA Modules:
  0.0 238.0 jit_solution(17940101722822431918)
XLA Ops:
  0.6 43.5 %plan_gathers.1 = (s32[4176,128]{1,0:T(8,128)S(1)}, f32[2832,128]{1,0:T(8,128)S(1)}, s32[64,128]{1,0:T(8,128)S(1)}, f32[8,128]{1,0:T(8,128)S(1)}) custom-call(s32[4,256]{1,0:T(4,128)} %send_c.1, s32[4,512]{1,0:T(4,128)} %send_e.1, s32[6,2048]{1,0:T(8,128)} %cell_edges.1, s32[6,2048]{1,0:T(8,128)} %cell_orient.1, s32[2,6144]{1,0:T(2,128)} %edge_cells.1, ...), custom_call_target="tpu_custom_call" | custom-call | tf_op jit(solution)/shard_map/plan_gathers/pallas_call | solution.py:547
  44.2 0.0 copy-start
  44.2 1.1 copy-done
  45.3 66.4 %psum.7 = f32[1,128]{1,0:T(1,128)S(1)} all-reduce(f32[1,128]{1,0:T(1,128)S(1)} %slice.186), channel_id=1, replica_groups=mesh['dom'=128] {'dom'}, use_global_device_ids=true, to_apply=%region_0.0 | all-reduce | flops 128 | bytes 1024 | tf_op jit(solution)/shard_map/psum | solution.py:560
  111.7 0.0 copy-start.1
  111.7 1.4 copy-done.1
  113.1 121.3 %three_sections.1 = (f32[16,2048]{1,0:T(8,128)}, f32[16,6144]{1,0:T(8,128)}) custom-call(f32[16,2048]{1,0:T(8,128)} %thickness.1, f32[16,6144]{1,0:T(8,128)} %velocity.1, s32[4176,128]{1,0:T(8,128)S(1)} %get-tuple-element.55.packed_in, f32[2832,128]{1,0:T(8,128)S(1)} %copy-done.1, f32[48,128]{1,0:T(8,128)} %bitcast.185, f32[48,128]{1,0:T(8,128)} %bitcast.186, ...), custom_call_target="tpu_custom_call" | custom-call | tf_op jit(solution)/shard_map/three_sections/pallas_call | solution.py:563
  234.4 0.2 conditional.1
  234.6 1.6 copy.359
  236.2 1.8 copy.360
  (1 shorter events, 0.0 us)
Async XLA Ops:
  44.2 1.1 copy-start
  111.7 1.4 copy-start.1

commit v3 on v2

--- a/solution.py
+++ b/solution.py
@@ -11,6 +11,7 @@
 mixing = 0.2
 time_step = 0.5
 LANES = 128
+TILES = 12
 OFFSETS = (-2, -1, 1, 2)
 VMEM = pltpu.VMEM
 SMEM = pltpu.SMEM
@@ -20,9 +21,10 @@
 class Plan:
     rows = weights = ids = 0
 
-    def __init__(self, terms, octets, first, chunks, cap, turns, cuts, weighted):
+    def __init__(self, terms, octets, first, chunks, cap, turns, weighted, apart):
         self.terms, self.octets, self.first, self.chunks = terms, octets, first, chunks
-        self.cap, self.turns, self.cuts, self.weighted = cap, turns, cuts, weighted
+        self.cap, self.turns, self.weighted, self.apart = cap, turns, weighted, apart
+        self.goals = 8 * terms if apart else 8
         self.row_at, self.weight_at, self.id_at = Plan.rows, Plan.weights, Plan.ids
         self.id_rows = -(-cap // LANES)
         Plan.rows += octets * cap
@@ -30,11 +32,11 @@
         Plan.ids += octets * self.id_rows
 
 
-AROUND = Plan(10, 6, 0, 48, 272, 4, 2, True), Plan(10, 6, 48, 16, 104, 2, 1, True)
-PAIR = Plan(1, 12, 0, 16, 56, 1, 1, False), Plan(1, 12, 16, 8, 32, 1, 1, False)
-SIDE = Plan(6, 2, 0, 48, 208, 4, 2, True), Plan(6, 2, 48, 16, 80, 2, 1, True)
-SEND_E = Plan(1, 2, 0, 48, 112, 2, 1, False)
-SEND_C = Plan(1, 1, 0, 16, 64, 1, 1, False)
+AROUND = Plan(10, 6, 0, 48, 272, 4, True, False), Plan(10, 6, 48, 16, 104, 2, True, False)
+PAIR = Plan(2, 6, 0, 16, 72, 1, False, True), Plan(2, 6, 16, 8, 40, 1, False, True)
+SIDE = Plan(6, 2, 0, 48, 208, 4, True, False), Plan(6, 2, 48, 16, 80, 2, True, False)
+SEND_E = Plan(1, 2, 0, 48, 112, 2, False, False)
+SEND_C = Plan(1, 1, 0, 16, 64, 1, False, False)
 ROWS, WEIGHTS, IDS = Plan.rows, Plan.weights, -(-Plan.ids // 8) * 8
 
 
@@ -71,8 +73,8 @@
         for k in range(plan.terms):
             chunks[k] = lax.shift_right_logical(raw[k, at, :], 7) - plan.first
 
-        def rank(k, counts):
-            counts = list(counts)
+        counts = [jnp.zeros((8, LANES), jnp.int32) for _ in range(tiles)]
+        for k in range(plan.terms):
             parts = []
             for s in range(8):
                 chunk = spread(chunks[k, s : s + 1, :])
@@ -84,9 +86,6 @@
                     counts[v] = jnp.where(hit, counts[v] + 1, counts[v])
                 parts.append(part)
             keys[k] = sums_of_rows(parts, sub)
-            return tuple(counts)
-
-        counts = lax.fori_loop(0, plan.terms, rank, tuple(jnp.zeros((8, LANES), jnp.int32) for _ in range(tiles)))
         most = [spread(jnp.max(c, axis=1, keepdims=True)) for c in counts]
         upto = most
         for shift in (1, 2, 4):
@@ -104,13 +103,13 @@
             inside = (chunk >= 0) & (chunk < plan.chunks)
             start = jnp.take_along_axis(starts, chunk & 127, axis=1, mode="promise_in_bounds")
             keys[k] = jnp.where(inside, start + keys[k], -1)
-            loads[k] = (raw[k, at, :] & 127) | (sub << 7) | (jnp.where(inside, chunk, 0) << 11)
+            loads[k] = (raw[k, at, :] & 127) | ((sub + 8 * k * plan.apart) << 7) | (jnp.where(inside, chunk, 0) << 12)
         places = [jnp.zeros((8, LANES), jnp.int32) for _ in range(plan.id_rows)]
-        size = plan.cap // 8 // plan.cuts
-        for cut in range(plan.cuts):
-            tops = [8 * (cut * size + v) for v in range(size)]
-
-            def match(k, found):
+        for top in range(0, plan.cap, 8 * TILES):
+            tops = list(range(top, min(top + 8 * TILES, plan.cap), 8))
+            size = len(tops)
+
+            def match(k, found, tops=tops, size=size):
                 load, weight = list(found[:size]), list(found[size:])
                 for s in range(8):
                     wanted = spread(keys[k, s : s + 1, :])
@@ -124,16 +123,16 @@
                             weight[v] = jnp.where(here, factor, weight[v])
                 return (*load, *weight)
 
-            begin = [jnp.full((8, LANES), 8 << 7, jnp.int32)] * size
+            begin = [jnp.full((8, LANES), 16 << 7, jnp.int32)] * size
             begin += [jnp.zeros((8, LANES), jnp.float32)] * (size * plan.weighted)
             found = lax.fori_loop(0, plan.terms, match, tuple(begin))
             for v in range(size):
                 load = found[v]
                 offset = o * plan.cap + tops[v]
-                packed[pl.ds(pl.multiple_of(plan.row_at + offset, 8), 8), :] = load & 2047
+                packed[pl.ds(pl.multiple_of(plan.row_at + offset, 8), 8), :] = load & 4095
                 if plan.weighted:
                     weights[pl.ds(pl.multiple_of(plan.weight_at + offset, 8), 8), :] = found[size + v]
-                own = jnp.max(load >> 11, axis=1, keepdims=True)
+                own = jnp.max(load >> 12, axis=1, keepdims=True)
                 which = tops[v] // LANES
                 places[which] = places[which] + jnp.where(lane == sub + tops[v] % LANES, own, 0)
         for i, place in enumerate(places):
@@ -158,8 +157,7 @@
             around[k, g : g + 1, :] = edge_edges[k : k + 1, at]
             factors[k, g : g + 1, :] = edge_weights[k : k + 1, at]
         for k in range(2):
-            to = g // 4 * 8 + k * 4 + g % 4
-            pair[0, to : to + 1, :] = edge_cells[k : k + 1, at]
+            pair[k, g : g + 1, :] = edge_cells[k : k + 1, at]
     for g in range(16):
         at = slice(g * LANES, (g + 1) * LANES)
         for k in range(6):
@@ -190,7 +188,7 @@
             if plan.weighted:
                 factor = spread(weights[pl.ds(plan.weight_at + at, 1), :])
                 found = [value * factor for value in found]
-            for d in range(8):
+            for d in range(plan.goals):
                 mine = goal == d
                 for i, value in enumerate(found):
                     j = d * len(sources) + i
@@ -215,10 +213,15 @@
 FIELDS = 3
 
 
-def step_kernel(thickness, velocity, packed_in, weights_in, spacing_in, length_in, coriolis_in, area_in, ids, *rest):
-    h_out, u_out = rest[:2]
-    (h0, u0, packed, weights, spacing, length, coriolis, area, loaded) = rest[2:11]
-    (h, u, flux, tangent, cells, spread_sum, send_h, send_u, send_f, halo_h, halo_u, halo_f, near, sent, came) = rest[11:]
+def partner(me, b):
+    return me + b - 2 * b * (me // b % 2)
+
+
+def step_kernel(thickness, velocity, packed_in, weights_in, spacing_in, length_in, coriolis_in, area_in, over, ids, *rest):
+    h_out, u_out, mark = rest[:3]
+    (h0, u0, packed, weights, spacing, length, coriolis, area, loaded) = rest[3:12]
+    (h, u, flux, tangent, cells, spread_sum, send_h, send_u, send_f, halo_h, halo_u, halo_f, near, sent, came) = rest[12:27]
+    told, heard, told_sem, heard_sem = rest[27:]
     me = lax.axis_index("dom")
     count = lax.axis_size("dom")
     barrier = pltpu.get_barrier_semaphore()
@@ -228,6 +231,32 @@
         @pl.when((peer >= 0) & (peer < count))
         def _():
             pl.semaphore_signal(barrier, inc=1, device_id=(peer,), device_id_type=pl.DeviceIdType.MESH)
+
+    rounds = count.bit_length() - 1
+    for r in range(2, rounds):
+        pl.semaphore_signal(barrier, inc=1, device_id=(partner(me, 2**r),), device_id_type=pl.DeviceIdType.MESH)
+    mark[...] = over[...]
+
+    def tell(r):
+        return pltpu.make_async_remote_copy(
+            src_ref=told.at[r],
+            dst_ref=heard.at[r],
+            send_sem=told_sem.at[r],
+            recv_sem=heard_sem.at[r],
+            device_id=(partner(me, lax.shift_left(1, r)),),
+            device_id_type=pl.DeviceIdType.MESH,
+        )
+
+    def spread_mark(r):
+        @pl.when((r >= 1) & (r <= rounds))
+        def _():
+            tell(r - 1).wait_recv()
+            mark[...] = jnp.maximum(mark[...], heard[r - 1])
+
+        @pl.when(r < rounds)
+        def _():
+            told[r] = mark[...]
+            tell(r).start()
 
     lists = (packed, weights, ids)
     given = (thickness, velocity, packed_in, spacing_in, length_in, coriolis_in, area_in, weights_in)
@@ -303,7 +332,7 @@
         h[group] = h0[:, group * LANES : (group + 1) * LANES]
     send_edges(0, (u, send_u))
     send_cells(0, h)
-    pl.semaphore_wait(barrier, jnp.minimum(me, 2) + jnp.minimum(count - 1 - me, 2))
+    pl.semaphore_wait(barrier, jnp.minimum(me, 2) + jnp.minimum(count - 1 - me, 2) + max(rounds - 2, 0))
     start(0, 0)
     start(1, 0)
     for i in range(3, len(copies)):
@@ -317,10 +346,10 @@
 
     def sweep(plan, take, ref, fresh):
         def octet(o, carry):
-            at = [o * 8 + d for d in range(8)]
-            begin = zeros(16) if fresh else [ref[a, rows, :] for a in at for rows in (TOP, LOW)]
+            at = [o * 8 + d % 8 + d // 8 * 48 for d in range(plan.goals)]
+            begin = zeros(2 * plan.goals) if fresh else [ref[a, rows, :] for a in at for rows in (TOP, LOW)]
             found = gather(plan, lists, o, both(take), begin)
-            for d in range(8):
+            for d in range(plan.goals):
                 for j, rows in enumerate((TOP, LOW)):
                     ref[at[d], rows, :] = found[2 * d + j]
             return carry
@@ -332,7 +361,7 @@
             for e in range(4):
                 group = q * 4 + e
                 at = lanes_at(group)
-                left, right = q * 8 + e, q * 8 + 4 + e
+                left, right = group, 48 + group
                 step = [cells[right, rows, :] - cells[left, rows, :] for rows in (TOP, LOW)]
                 mean = [0.5 * (cells[right, rows, :] + cells[left, rows, :]) for rows in (TOP, LOW)]
                 column = [running(x) for x in step]
@@ -359,12 +388,14 @@
 
     def section(k, carry):
         tau = time_step / (3 - k).astype(jnp.float32)
+        spread_mark(3 * k)
         sweep(AROUND[0], table(u), tangent, True)
         sweep(PAIR[0], table(h), cells, True)
         arrive(1, k)
         sweep(AROUND[1], table(near), tangent, False)
         arrive(0, k)
         sweep(PAIR[1], table(near), cells, False)
+        spread_mark(3 * k + 1)
         edges_of(k, tau)
 
         later = jnp.minimum(k + 1, 2)
@@ -381,6 +412,7 @@
             start(2, 2)
 
         sweep(SIDE[0], table(flux), spread_sum, True)
+        spread_mark(3 * k + 2)
         arrive(2, k)
         sweep(SIDE[1], table(near), spread_sum, False)
         for group in range(16):
@@ -415,6 +447,8 @@
         u_out[:, group * LANES : (group + 1) * LANES] = u[group]
     for group in range(16):
         h_out[:, group * LANES : (group + 1) * LANES] = h[group]
+    for r in range(rounds):
+        tell(r).wait_send()
     for field in range(FIELDS):
         for k in range(3):
             for place, offset in enumerate(OFFSETS):
@@ -552,34 +586,35 @@
         out_specs=whole(4),
         scratch_shapes=held(jnp.int32, around)
         + held(jnp.float32, around)
-        + held(jnp.int32, (1, 96, LANES), side)
+        + held(jnp.int32, (2, 48, LANES), side)
         + held(jnp.float32, side)
         + held(jnp.int32, (1, 16, LANES), (1, 8, LANES), *[(10, 8, LANES)] * 3),
         compiler_params=pltpu.CompilerParams(vmem_limit_bytes=24 << 20),
     )(*index, edge_weights)
-    overs = lax.psum(over[:1], "dom")[0, 0]
     coefs = [x.reshape(48, LANES) for x in (edge_spacing, edge_length, coriolis)] + [cell_area.reshape(16, LANES)]
     rows, groups, halo = (48, LANES), (48, 16, LANES), (3, 16, 16, LANES)
-    fast = pl.pallas_call(
+    h, u, mark = pl.pallas_call(
         step_kernel,
         name="three_sections",
-        in_specs=[pl.BlockSpec(memory_space=pl.ANY)] * 8 + [pl.BlockSpec(memory_space=SMEM)],
-        out_shape=[floats(16, 16 * LANES), floats(16, 48 * LANES)],
-        out_specs=whole(2),
+        in_specs=[pl.BlockSpec(memory_space=pl.ANY)] * 8 + whole(1) + [pl.BlockSpec(memory_space=SMEM)],
+        out_shape=[floats(16, 16 * LANES), floats(16, 48 * LANES), floats(8, LANES)],
+        out_specs=whole(3),
         scratch_shapes=held(jnp.float32, (16, 16 * LANES), (16, 48 * LANES))
         + held(jnp.int32, (ROWS, LANES))
         + held(jnp.float32, (WEIGHTS, LANES), rows, rows, rows, (16, LANES))
         + [pltpu.SemaphoreType.DMA((8,))]
         + held(jnp.float32, (16, 16, LANES), groups, groups, groups, (96, 16, LANES), (16, 16, LANES))
         + held(jnp.float32, (3, 8, 16, LANES), halo, halo, (3, 8, 16, LANES), halo, halo, (16, 16, LANES))
-        + [pltpu.SemaphoreType.DMA((3, FIELDS, 4)), pltpu.SemaphoreType.DMA((3, FIELDS, 4))],
+        + [pltpu.SemaphoreType.DMA((3, FIELDS, 4)), pltpu.SemaphoreType.DMA((3, FIELDS, 4))]
+        + held(jnp.float32, (7, 8, LANES), (7, 8, LANES))
+        + [pltpu.SemaphoreType.DMA((7,)), pltpu.SemaphoreType.DMA((7,))],
         compiler_params=pltpu.CompilerParams(collective_id=0, has_side_effects=True, vmem_limit_bytes=32 << 20),
-    )(thickness, velocity, packed, weights, *coefs, ids)
+    )(thickness, velocity, packed, weights, *coefs, over, ids)
 
     def in_general():
         return general(thickness, velocity, *index, edge_weights, cell_area, edge_spacing, edge_length, coriolis)
 
-    return lax.cond(overs > 0, in_general, lambda: tuple(fast))
+    return lax.cond(mark[0, 0] > 0, in_general, lambda: (h, u))
 
 
 def solution(mesh):

time: 238 us -> 168 us (0.71)
  blocking collectives: 66.4 us -> 0 us
  Pallas kernels: 165 us -> 162 us
    psum x1 -> x0, blocking collectives: 66.4 us -> none  [shards(): overs = lax.psum(over[:1], 'dom')[0, 0]]
    pallas_call x1, Pallas kernels: 43.5 us -> 39.3 us  [shards(): pl.pallas_call(plans_kernel, name='plan_gathers', in_specs=whole(7), out_...]
    unnamed x6 -> x2, local copies, waits for them, and re-layouts: 5.81 us -> 3.34 us
where the time goes in v3:
time: 168 us; the launch traced here: 167 us
  Pallas kernels  162 us (96%)
  local copies, waits for them, and re-layouts  3.85 us (2%)
    pallas_call x1, Pallas kernels, shards(): pl.pallas_call(step_kernel, name='three_sections', in_specs=[pl.BlockSpec...  122 us
    pallas_call x1, Pallas kernels, shards(): pl.pallas_call(plans_kernel, name='plan_gathers', in_specs=whole(7), out_...  39.3 us

profile of v3, /device:TPU:9, one launch (start us, length us, event | category | flops | bytes accessed | tf_op | source)
XLA Modules:
  0.0 167.0 jit_solution(12130757691599882782)
XLA Ops:
  0.6 39.3 %plan_gathers.1 = (s32[3792,128]{1,0:T(8,128)S(1)}, f32[2832,128]{1,0:T(8,128)S(1)}, s32[48,128]{1,0:T(8,128)S(1)}, f32[8,128]{1,0:T(8,128)S(1)}) custom-call(s32[4,256]{1,0:T(4,128)} %send_c.1, s32[4,512]{1,0:T(4,128)} %send_e.1, s32[6,2048]{1,0:T(8,128)} %cell_edges.1, s32[6,2048]{1,0:T(8,128)} %cell_orient.1, s32[2,6144]{1,0:T(2,128)} %edge_cells.1, ...), custom_call_target="tpu_custom_call" | custom-call | tf_op jit(solution)/shard_map/plan_gathers/pallas_call | solution.py:581
  40.0 122.3 %three_sections.1 = (f32[16,2048]{1,0:T(8,128)}, f32[16,6144]{1,0:T(8,128)}, f32[8,128]{1,0:T(8,128)S(1)}) custom-call(f32[16,2048]{1,0:T(8,128)} %thickness.1, f32[16,6144]{1,0:T(8,128)} %velocity.1, s32[3792,128]{1,0:T(8,128)S(1)} %get-tuple-element.57.packed_in, f32[2832,128]{1,0:T(8,128)S(1)} %get-tuple-element.58.weights_in, f32[48,128]{1,0:T(8,128)} %bitcast.184, ...), custom_call_target="tpu_custom_call" | custom-call | tf_op jit(solution)/shard_map/three_sections/pallas_call | solution.py:596
  162.3 0.5 slice.183
  163.4 0.2 conditional.1
  163.7 1.6 copy.359
  165.2 1.8 %copy.360 = f32[16,6144]{1,0:T(8,128)} copy(f32[16,6144]{1,0:T(8,128)} %get-tuple-element.261) | data formatting | bytes 786432

commit v4 on v3

--- a/solution.py
+++ b/solution.py
@@ -26,15 +26,15 @@
         self.cap, self.turns, self.weighted, self.apart = cap, turns, weighted, apart
         self.goals = 8 * terms if apart else 8
         self.row_at, self.weight_at, self.id_at = Plan.rows, Plan.weights, Plan.ids
-        self.id_rows = -(-cap // LANES)
-        Plan.rows += octets * cap
-        Plan.weights += octets * cap * weighted
-        Plan.ids += octets * self.id_rows
-
-
-AROUND = Plan(10, 6, 0, 48, 272, 4, True, False), Plan(10, 6, 48, 16, 104, 2, True, False)
+        self.tiles, self.steps = cap // 8, cap // turns
+        Plan.rows += octets * self.tiles
+        Plan.weights += octets * self.tiles * weighted
+        Plan.ids += octets * turns
+
+
+AROUND = Plan(10, 6, 0, 48, 280, 5, True, False), Plan(10, 6, 48, 16, 104, 1, True, False)
 PAIR = Plan(2, 6, 0, 16, 72, 1, False, True), Plan(2, 6, 16, 8, 40, 1, False, True)
-SIDE = Plan(6, 2, 0, 48, 208, 4, True, False), Plan(6, 2, 48, 16, 80, 2, True, False)
+SIDE = Plan(6, 2, 0, 48, 208, 2, True, False), Plan(6, 2, 48, 16, 80, 1, True, False)
 SEND_E = Plan(1, 2, 0, 48, 112, 2, False, False)
 SEND_C = Plan(1, 1, 0, 16, 64, 1, False, False)
 ROWS, WEIGHTS, IDS = Plan.rows, Plan.weights, -(-Plan.ids // 8) * 8
@@ -104,7 +104,7 @@
             start = jnp.take_along_axis(starts, chunk & 127, axis=1, mode="promise_in_bounds")
             keys[k] = jnp.where(inside, start + keys[k], -1)
             loads[k] = (raw[k, at, :] & 127) | ((sub + 8 * k * plan.apart) << 7) | (jnp.where(inside, chunk, 0) << 12)
-        places = [jnp.zeros((8, LANES), jnp.int32) for _ in range(plan.id_rows)]
+        places = [jnp.zeros((8, LANES), jnp.int32) for _ in range(plan.turns)]
         for top in range(0, plan.cap, 8 * TILES):
             tops = list(range(top, min(top + 8 * TILES, plan.cap), 8))
             size = len(tops)
@@ -128,15 +128,15 @@
             found = lax.fori_loop(0, plan.terms, match, tuple(begin))
             for v in range(size):
                 load = found[v]
-                offset = o * plan.cap + tops[v]
-                packed[pl.ds(pl.multiple_of(plan.row_at + offset, 8), 8), :] = load & 4095
+                offset = o * plan.tiles + tops[v] // 8
+                packed[plan.row_at + offset] = load & 4095
                 if plan.weighted:
-                    weights[pl.ds(pl.multiple_of(plan.weight_at + offset, 8), 8), :] = found[size + v]
+                    weights[plan.weight_at + offset] = found[size + v]
                 own = jnp.max(load >> 12, axis=1, keepdims=True)
-                which = tops[v] // LANES
-                places[which] = places[which] + jnp.where(lane == sub + tops[v] % LANES, own, 0)
+                which, lane_at = divmod(tops[v], plan.steps)
+                places[which] = places[which] + jnp.where(lane == sub + lane_at, own, 0)
         for i, place in enumerate(places):
-            ids[pl.ds(plan.id_at + o * plan.id_rows + i, 1), :] = jnp.sum(place, axis=0, keepdims=True)
+            ids[pl.ds(plan.id_at + o * plan.turns + i, 1), :] = jnp.sum(place, axis=0, keepdims=True)
         return carry
 
     lax.fori_loop(0, plan.octets, octet, 0)
@@ -174,19 +174,18 @@
 
 def gather(plan, lists, o, sources, sums):
     packed, weights, ids = lists
-    steps = plan.cap // plan.turns
 
     def step(t, sums):
         sums = list(sums)
-        for r in range(steps):
-            row = t * steps + r
-            at = o * plan.cap + row
-            chunk = ids[plan.id_at + o * plan.id_rows + row // LANES, row % LANES]
-            load = spread(packed[pl.ds(plan.row_at + at, 1), :])
+        turn_at = o * plan.turns + t
+        tile_at = turn_at * (plan.steps // 8)
+        for r in range(plan.steps):
+            chunk = ids[plan.id_at + turn_at, r]
+            load = spread(packed[plan.row_at + tile_at + r // 8, r % 8 : r % 8 + 1, :])
             pick, goal = load & 127, lax.shift_right_logical(load, 7)
             found = [jnp.take_along_axis(take(chunk), pick, axis=1, mode="promise_in_bounds") for take in sources]
             if plan.weighted:
-                factor = spread(weights[pl.ds(plan.weight_at + at, 1), :])
+                factor = spread(weights[plan.weight_at + tile_at + r // 8, r % 8 : r % 8 + 1, :])
                 found = [value * factor for value in found]
             for d in range(plan.goals):
                 mine = goal == d
@@ -582,7 +581,7 @@
         plans_kernel,
         name="plan_gathers",
         in_specs=whole(7),
-        out_shape=[ints(ROWS, LANES), floats(WEIGHTS, LANES), ints(IDS, LANES), floats(8, LANES)],
+        out_shape=[ints(ROWS, 8, LANES), floats(WEIGHTS, 8, LANES), ints(IDS, LANES), floats(8, LANES)],
         out_specs=whole(4),
         scratch_shapes=held(jnp.int32, around)
         + held(jnp.float32, around)
@@ -600,8 +599,8 @@
         out_shape=[floats(16, 16 * LANES), floats(16, 48 * LANES), floats(8, LANES)],
         out_specs=whole(3),
         scratch_shapes=held(jnp.float32, (16, 16 * LANES), (16, 48 * LANES))
-        + held(jnp.int32, (ROWS, LANES))
-        + held(jnp.float32, (WEIGHTS, LANES), rows, rows, rows, (16, LANES))
+        + held(jnp.int32, (ROWS, 8, LANES))
+        + held(jnp.float32, (WEIGHTS, 8, LANES), rows, rows, rows, (16, LANES))
         + [pltpu.SemaphoreType.DMA((8,))]
         + held(jnp.float32, (16, 16, LANES), groups, groups, groups, (96, 16, LANES), (16, 16, LANES))
         + held(jnp.float32, (3, 8, 16, LANES), halo, halo, (3, 8, 16, LANES), halo, halo, (16, 16, LANES))

time: 168 us -> 151 us (0.90)
  Pallas kernels: 162 us -> 145 us
    pallas_call x1, Pallas kernels: 122 us -> 106 us  [shards(): pl.pallas_call(step_kernel, name='three_sections', in_specs=[pl.BlockSpec...]
where the time goes in v4:
time: 151 us
  Pallas kernels  145 us (96%)
  local copies, waits for them, and re-layouts  3.85 us (3%)
    pallas_call x1, Pallas kernels, shards(): pl.pallas_call(step_kernel, name='three_sections', in_specs=[pl.BlockSpec...  106 us
    pallas_call x1, Pallas kernels, shards(): pl.pallas_call(plans_kernel, name='plan_gathers', in_specs=whole(7), out_...  39.6 us
    unnamed x2, local copies, waits for them, and re-layouts  3.34 us

profile of v4, /device:TPU:9, one launch (start us, length us, event | category | flops | bytes accessed | tf_op | source)
XLA Modules:
  0.0 150.6 jit_solution(5136471812721938683)
XLA Ops:
  0.6 39.6 %plan_gathers.1 = (s32[480,8,128]{2,1,0:T(8,128)S(1)}, f32[360,8,128]{2,1,0:T(8,128)S(1)}, s32[64,128]{1,0:T(8,128)S(1)}, f32[8,128]{1,0:T(8,128)S(1)}) custom-call(s32[4,256]{1,0:T(4,128)} %send_c.1, s32[4,512]{1,0:T(4,128)} %send_e.1, s32[6,2048]{1,0:T(8,128)} %cell_edges.1, s32[6,2048]{1,0:T(8,128)} %cell_orient.1, s32[2,6144]{1,0:T(2,128)} %edge_cells.1, ...), custom_call_target="tpu_custom_call" | custom-call | tf_op jit(solution)/shard_map/plan_gathers/pallas_call | solution.py:580
  40.2 105.6 %three_sections.1 = (f32[16,2048]{1,0:T(8,128)}, f32[16,6144]{1,0:T(8,128)}, f32[8,128]{1,0:T(8,128)S(1)}) custom-call(f32[16,2048]{1,0:T(8,128)} %thickness.1, f32[16,6144]{1,0:T(8,128)} %velocity.1, s32[480,8,128]{2,1,0:T(8,128)S(1)} %get-tuple-element.57.packed_in, f32[360,8,128]{2,1,0:T(8,128)S(1)} %get-tuple-element.58.weights_in, f32[48,128]{1,0:T(8,128)} %bitcast.184, ...), custom_call_target="tpu_custom_call" | custom-call | tf_op jit(solution)/shard_map/three_sections/pallas_call | solution.py:595
  145.8 0.5 slice.183
  147.0 0.2 conditional.1
  147.2 1.6 %copy.359 = f32[16,2048]{1,0:T(8,128)} copy(f32[16,2048]{1,0:T(8,128)} %get-tuple-element.260) | data formatting | bytes 262144
  148.8 1.8 %copy.360 = f32[16,6144]{1,0:T(8,128)} copy(f32[16,6144]{1,0:T(8,128)} %get-tuple-element.261) | data formatting | bytes 786432
